TPU v7x, 32 devices: a whole 2x2x4 slice. The times are simulated.
32 devices in a mesh: section: 8 (over y, x, core), dp: 4 (over z).
Axes of the slice: x: 2, y: 2, z: 4, core: 2. Of those that a mesh axis runs over, the one named last changes fastest.
Arguments:
- token_ids: int32 [8, 4, 256], P(None, 'dp'), may hold values from 0 to 26
- order: int32 [8, 4, 256], P(None, 'dp'), may hold values from 0 to 255, each once within a row
- timesteps: int32 [8, 4], P(None, 'dp'), may hold values from 0 to 255
- table: float32 [28, 512], replicated, may hold values from -0.5 to 0.5
- norm_gain: float32 [8, 2, 512], P('section', None, 'dp'), may hold values from 0.5 to 1.5
- norm_bias: float32 [8, 2, 512], P('section', None, 'dp'), may hold values from -1.8 to 1.8
- w_qkv: float32 [8, 512, 1536], P('section', 'dp'), may hold values from -0.25 to 0.25
- w_out: float32 [8, 512, 512], P('section', 'dp'), may hold values from -1 to 1
- w_in: float32 [8, 512, 2048], P('section', 'dp'), may hold values from -0.25 to 0.25
- w_down: float32 [8, 2048, 512], P('section', 'dp'), may hold values from -0.125 to 0.125
Outputs:
- table_grad: float32 [28, 512], P(None, 'section')
- gain_grad: float32 [8, 2, 512], P('section', None, 'dp')
- bias_grad: float32 [8, 2, 512], P('section', None, 'dp')
- w_qkv_grad: float32 [8, 512, 1536], P('section', 'dp')
- w_out_grad: float32 [8, 512, 512], P('section', 'dp')
- w_in_grad: float32 [8, 512, 2048], P('section', 'dp')
- w_down_grad: float32 [8, 2048, 512], P('section', 'dp')
All inputs are finite; a program needn't handle non-finite values.
Results may differ from a plain program's by a relative error of at most 0.012.
The roundings to bfloat16 on the way count: a program that leaves them out, or rounds other values in their place, can miss the bound.
Values may be sent and summed in bfloat16 or wider, within the bound.
A program may use at most 128 MiB of HBM per device.

v0:
```python
import math

import jax
import jax.numpy as jnp
from jax import lax
from jax.sharding import PartitionSpec as P

HEADS = 8


EPSILON = 1e-05
EMBED_GAIN = 16.0


def shifted_2(block, axis, distance):
    devices = range(lax.axis_size(axis))
    route = [(i - distance, i) for i in devices if i - distance in devices]
    return lax.ppermute(block, axis, route)


def shortened(shard):
    return jax.tree.map(lambda a: a.astype(jnp.bfloat16) if a.dtype == jnp.float32 else a, shard)


def unit_rows(values):
    average = jnp.mean(values, axis=-1, keepdims=True)
    centered = values - average
    variance = jnp.mean(centered * centered, axis=-1, keepdims=True)
    return centered * lax.rsqrt(variance + EPSILON)


def row_norm(values, gain_row, offset):
    return unit_rows(values) * gain_row + offset


def matmul_rows(left, right):
    return jnp.einsum("btd,de->bte", left, right, preferred_element_type=jnp.float32)


def matmul_back(gradient, right):
    return jnp.einsum("bte,de->btd", gradient, right, preferred_element_type=jnp.float32)


def outer_sum(left, gradient):
    return jnp.einsum("btd,bte->de", left, gradient, preferred_element_type=jnp.float32)


def layer_forward(hidden, weights):
    gain_pair, bias_pair, w_qkv, w_out, w_in, w_down = weights
    seq_count, length, model_width = hidden.shape
    head_size = model_width // HEADS
    score_scale = 1.0 / math.sqrt(head_size)
    normed = row_norm(
        hidden, gain_pair[0].astype(jnp.float32), bias_pair[0].astype(jnp.float32)
    ).astype(jnp.bfloat16)
    packed = matmul_rows(normed, w_qkv).astype(jnp.bfloat16)
    heads_view = packed.reshape(seq_count, length, 3, HEADS, head_size)
    scores = (
        jnp.einsum(
            "bqhe,bkhe->bhqk",
            heads_view[:, :, 0],
            heads_view[:, :, 1],
            preferred_element_type=jnp.float32,
        )
        * score_scale
    )
    attention = jax.nn.softmax(scores, axis=-1)
    mixed_rows = jnp.einsum(
        "bhqk,bkhe->bqhe",
        attention.astype(jnp.bfloat16),
        heads_view[:, :, 2],
        preferred_element_type=jnp.float32,
    )
    mixed_rows = mixed_rows.astype(jnp.bfloat16).reshape(seq_count, length, model_width)
    middle = hidden + matmul_rows(mixed_rows, w_out)
    normed_two = row_norm(
        middle, gain_pair[1].astype(jnp.float32), bias_pair[1].astype(jnp.float32)
    ).astype(jnp.bfloat16)
    lifted = matmul_rows(normed_two, w_in)
    activated = jax.nn.gelu(lifted).astype(jnp.bfloat16)
    output = middle + matmul_rows(activated, w_down)
    return (
        output.astype(jnp.bfloat16),
        (hidden, normed, packed, attention, mixed_rows, middle, normed_two, lifted, activated),
    )


def layer_backward(kept_values, weights, grad_out):
    hidden, normed, packed, attention, mixed_rows, middle, normed_two, lifted, activated = (
        kept_values
    )
    gain_pair, bias_pair, w_qkv, w_out, w_in, w_down = weights
    seq_count, length, model_width = hidden.shape
    head_size = model_width // HEADS
    score_scale = 1.0 / math.sqrt(head_size)
    grad_branch = grad_out.astype(jnp.bfloat16)
    grad_down = jnp.einsum(
        "btf,btd->fd", activated, grad_branch, preferred_element_type=jnp.float32
    )
    grad_active = jnp.einsum("btd,fd->btf", grad_branch, w_down, preferred_element_type=jnp.float32)
    _, gelu_pull = jax.vjp(jax.nn.gelu, lifted)
    grad_lifted = gelu_pull(grad_active)[0].astype(jnp.bfloat16)
    grad_in = outer_sum(normed_two, grad_lifted)
    grad_normed_two = matmul_back(grad_lifted, w_in)
    _, norm_pull_two = jax.vjp(
        row_norm, middle, gain_pair[1].astype(jnp.float32), bias_pair[1].astype(jnp.float32)
    )
    grad_middle, gain_two, bias_two = norm_pull_two(grad_normed_two)
    grad_middle = grad_middle + grad_out
    grad_attended = grad_middle.astype(jnp.bfloat16)
    grad_out_proj = outer_sum(mixed_rows, grad_attended)
    grad_mixed = (
        matmul_back(grad_attended, w_out)
        .astype(jnp.bfloat16)
        .reshape(seq_count, length, HEADS, head_size)
    )
    heads_view = packed.reshape(seq_count, length, 3, HEADS, head_size)
    query_rows, key_rows, value_rows = (
        heads_view[:, :, 0],
        heads_view[:, :, 1],
        heads_view[:, :, 2],
    )
    grad_attention = jnp.einsum(
        "bqhe,bkhe->bhqk", grad_mixed, value_rows, preferred_element_type=jnp.float32
    )
    grad_values = jnp.einsum(
        "bhqk,bqhe->bkhe",
        attention.astype(jnp.bfloat16),
        grad_mixed,
        preferred_element_type=jnp.float32,
    )
    grad_scores = attention * (
        grad_attention - jnp.sum(attention * grad_attention, axis=-1, keepdims=True)
    )
    grad_scores = grad_scores.astype(jnp.bfloat16)
    grad_queries = (
        jnp.einsum("bhqk,bkhe->bqhe", grad_scores, key_rows, preferred_element_type=jnp.float32)
        * score_scale
    )
    grad_keys = (
        jnp.einsum("bhqk,bqhe->bkhe", grad_scores, query_rows, preferred_element_type=jnp.float32)
        * score_scale
    )
    grad_packed = jnp.stack([grad_queries, grad_keys, grad_values], axis=2)
    grad_packed = grad_packed.reshape(seq_count, length, 3 * model_width).astype(jnp.bfloat16)
    grad_qkv = outer_sum(normed, grad_packed)
    grad_normed = matmul_back(grad_packed, w_qkv)
    _, norm_pull_one = jax.vjp(
        row_norm, hidden, gain_pair[0].astype(jnp.float32), bias_pair[0].astype(jnp.float32)
    )
    grad_hidden, gain_one, bias_one = norm_pull_one(grad_normed)
    layer_terms = (
        jnp.stack([gain_one, gain_two]),
        jnp.stack([bias_one, bias_two]),
        grad_qkv,
        grad_out_proj,
        grad_in,
        grad_down,
    )
    return (grad_hidden + grad_middle, layer_terms)


def section_forward(hidden, gathered):
    weights = tuple((tensor[0] for tensor in gathered))
    rounded, kept_values = layer_forward(hidden, weights)
    kept_layers = [kept_values]
    return (rounded, tuple(kept_layers))


def section_backward(kept_layers, gathered, grad_top):
    layer_count = len(kept_layers)
    grad_hidden = grad_top
    grad_layers = []
    for layer_index in reversed(range(layer_count)):
        weights = tuple((tensor[layer_index] for tensor in gathered))
        if layer_index < layer_count - 1:
            grad_hidden = lax.optimization_barrier(grad_hidden.astype(jnp.bfloat16)).astype(
                jnp.float32
            )
        grad_hidden, layer_terms = layer_backward(kept_layers[layer_index], weights, grad_hidden)
        grad_layers.insert(0, layer_terms)
    stacked = tuple((jnp.stack([terms[member] for terms in grad_layers]) for member in range(6)))
    return (grad_hidden, stacked)


def head_step(outgoing, table_low, target_ids, weight_rows, letters):
    normalized, unit_pull = jax.vjp(unit_rows, outgoing.astype(jnp.float32))
    normalized_low = normalized.astype(jnp.bfloat16)
    logits = jnp.einsum(
        "vd,btd->bvt", table_low, normalized_low, preferred_element_type=jnp.float32
    )
    largest = jnp.max(logits, axis=1, keepdims=True)
    shifted = jnp.exp(logits - largest)
    totals = jnp.sum(shifted, axis=1, keepdims=True)
    target_hot = (target_ids[:, None, :] == letters).astype(jnp.float32)
    grad_logits = (weight_rows[:, None, :] * (shifted / totals - target_hot)).astype(jnp.bfloat16)
    grad_normalized = jnp.einsum(
        "bvt,vd->btd", grad_logits, table_low, preferred_element_type=jnp.float32
    )
    table_term = jnp.einsum(
        "bvt,btd->vd", grad_logits, normalized_low, preferred_element_type=jnp.float32
    )
    grad_final = unit_pull(grad_normalized)[0]
    return (grad_final.astype(jnp.bfloat16), table_term)


def body(token_ids, order, timesteps, table, norm_gain, norm_bias, w_qkv, w_out, w_in, w_down):
    section_count = lax.axis_size("section")
    section_at = lax.axis_index("section")
    last_section = section_count - 1
    micro_count, seq_count, length = token_ids.shape
    vocab_size, model_width = table.shape
    step_count = micro_count + section_count - 1
    visible = order < timesteps[:, :, None]
    shown = jnp.where(visible, token_ids, vocab_size - 1)
    loss_weight = jnp.where(visible, 0.0, 1.0) / (length - timesteps)[:, :, None].astype(
        jnp.float32
    )
    letters = lax.broadcasted_iota(jnp.int32, (1, vocab_size, 1), 1)
    table_low = table.astype(jnp.bfloat16)
    gathered = (
        lax.all_gather(norm_gain.astype(jnp.bfloat16), "dp", axis=2, tiled=True),
        lax.all_gather(norm_bias.astype(jnp.bfloat16), "dp", axis=2, tiled=True),
        lax.all_gather(w_qkv.astype(jnp.bfloat16), "dp", axis=1, tiled=True),
        lax.all_gather(w_out.astype(jnp.bfloat16), "dp", axis=1, tiled=True),
        lax.all_gather(w_in.astype(jnp.bfloat16), "dp", axis=1, tiled=True),
        lax.all_gather(w_down.astype(jnp.bfloat16), "dp", axis=1, tiled=True),
    )
    zeros_rows = jnp.zeros((seq_count, length, model_width), jnp.bfloat16)

    def one_hot_rows(slot_index):
        chosen = lax.dynamic_index_in_dim(shown, slot_index, 0, keepdims=False)
        return (chosen[:, None, :] == letters).astype(jnp.float32)

    def forward_step(step_index, loop_state):
        micro_index = step_index - section_at
        active = jnp.logical_and(micro_index >= 0, micro_index < micro_count)
        slot_index = jnp.clip(micro_index, 0, micro_count - 1)

        def forward_work(loop_values):
            incoming, inputs_store, grad_store, kept_store, table_sum = loop_values
            embedded = (
                jnp.einsum(
                    "bvt,vd->btd", one_hot_rows(slot_index), table, precision=lax.Precision.HIGHEST
                )
                * EMBED_GAIN
            )
            section_input = jnp.where(section_at == 0, embedded, incoming.astype(jnp.float32))
            outgoing, kept_layers = section_forward(section_input, gathered)
            inputs_store = lax.dynamic_update_index_in_dim(
                inputs_store, section_input, slot_index, 0
            )
            target_ids = lax.dynamic_index_in_dim(token_ids, slot_index, 0, keepdims=False)
            weight_rows = lax.dynamic_index_in_dim(loss_weight, slot_index, 0, keepdims=False)
            grad_final, table_term = head_step(
                outgoing, table_low, target_ids, weight_rows, letters
            )
            on_last = section_at == last_section
            table_sum = table_sum + jnp.where(on_last, table_term, 0.0)
            grad_store = lax.dynamic_update_index_in_dim(grad_store, grad_final, slot_index, 0)
            return (outgoing, inputs_store, grad_store, kept_store, table_sum)

        def forward_skip(loop_values):
            return (zeros_rows,) + tuple(loop_values[1:])

        result = lax.cond(active, forward_work, forward_skip, loop_state)
        incoming = shifted_2(result[0], "section", 1)
        return (incoming,) + tuple(result[1:])

    kept_initial = ()
    forward_initial = (
        zeros_rows,
        jnp.zeros((micro_count, seq_count, length, model_width), jnp.float32),
        jnp.zeros((micro_count, seq_count, length, model_width), jnp.bfloat16),
        kept_initial,
        jnp.zeros((vocab_size, model_width), jnp.float32),
    )
    forward_done = lax.fori_loop(0, step_count, forward_step, forward_initial)
    inputs_store, grad_store, kept_store, table_head = forward_done[1:]

    def backward_step(step_index, loop_state):
        micro_index = step_index - (last_section - section_at)
        active = jnp.logical_and(micro_index >= 0, micro_index < micro_count)
        slot_index = jnp.clip(micro_index, 0, micro_count - 1)

        def backward_work(loop_values):
            incoming, grad_sums, table_embed = loop_values
            from_head = lax.dynamic_index_in_dim(grad_store, slot_index, 0, keepdims=False)
            grad_top = jnp.where(section_at == last_section, from_head, incoming).astype(
                jnp.float32
            )
            section_input = lax.dynamic_index_in_dim(inputs_store, slot_index, 0, keepdims=False)
            kept_layers = section_forward(section_input, gathered)[1]
            grad_input, layer_terms = section_backward(kept_layers, gathered, grad_top)
            grad_sums = tuple((before + term for before, term in zip(grad_sums, layer_terms)))
            embed_term = (
                jnp.einsum(
                    "bvt,btd->vd",
                    one_hot_rows(slot_index),
                    grad_input,
                    precision=lax.Precision.HIGHEST,
                )
                * EMBED_GAIN
            )
            table_embed = table_embed + jnp.where(section_at == 0, embed_term, 0.0)
            return (grad_input.astype(jnp.bfloat16), grad_sums, table_embed)

        def backward_skip(loop_values):
            return (zeros_rows,) + tuple(loop_values[1:])

        result = lax.cond(active, backward_work, backward_skip, loop_state)
        incoming = shifted_2(shortened(result[0]), "section", -1)
        return (incoming,) + tuple(result[1:])

    sums_initial = tuple((jnp.zeros(tensor.shape, jnp.float32) for tensor in gathered))
    backward_initial = (zeros_rows, sums_initial, jnp.zeros((vocab_size, model_width), jnp.float32))
    backward_done = lax.fori_loop(0, step_count, backward_step, backward_initial)
    grad_sums, table_embed = (backward_done[1], backward_done[2])
    gain_sum, bias_sum, qkv_sum, out_sum, in_sum, down_sum = (
        lax.psum_scatter(
            grad_sums[0].astype(jnp.bfloat16), "dp", scatter_dimension=2, tiled=True
        ).astype(jnp.float32),
        lax.psum_scatter(
            grad_sums[1].astype(jnp.bfloat16), "dp", scatter_dimension=2, tiled=True
        ).astype(jnp.float32),
        lax.psum_scatter(
            grad_sums[2].astype(jnp.bfloat16), "dp", scatter_dimension=1, tiled=True
        ).astype(jnp.float32),
        lax.psum_scatter(
            grad_sums[3].astype(jnp.bfloat16), "dp", scatter_dimension=1, tiled=True
        ).astype(jnp.float32),
        lax.psum_scatter(
            grad_sums[4].astype(jnp.bfloat16), "dp", scatter_dimension=1, tiled=True
        ).astype(jnp.float32),
        lax.psum_scatter(
            grad_sums[5].astype(jnp.bfloat16), "dp", scatter_dimension=1, tiled=True
        ).astype(jnp.float32),
    )
    table_part = lax.psum_scatter(
        (table_head + table_embed).astype(jnp.bfloat16), "section", scatter_dimension=1, tiled=True
    ).astype(jnp.float32)
    table_total = lax.psum(table_part, "dp")
    return (table_total, gain_sum, bias_sum, qkv_sum, out_sum, in_sum, down_sum)


def solution(mesh):
    in_specs = (
        P(None, "dp", None),
        P(None, "dp", None),
        P(None, "dp"),
        P(),
        P("section", None, "dp"),
        P("section", None, "dp"),
        P("section", "dp", None),
        P("section", "dp", None),
        P("section", "dp", None),
        P("section", "dp", None),
    )
    out_specs = (
        P(None, "section"),
        P("section", None, "dp"),
        P("section", None, "dp"),
        P("section", "dp", None),
        P("section", "dp", None),
        P("section", "dp", None),
        P("section", "dp", None),
    )
    return jax.shard_map(body, mesh=mesh, in_specs=in_specs, out_specs=out_specs, check_vma=False)
```

profile of v0, /device:TPU:1, one launch (start us, length us, event | category | flops | bytes accessed | tf_op | source)
XLA Modules:
  0.0 1661.2 jit_solution(18288006356024382805)
XLA Ops:
  11.4 9.9 all_gather.19
  27.3 19.6 %all_gather.21 = bf16[1,512,512]{2,1,0:T(8,128)(2,1)} all-gather(bf16[1,128,512]{2,1,0:T(8,128)(2,1)S(1)} %convert_element_type.287), channel_id=1, replica_groups=mesh['section'=8,'dp'=4] {'dp'}, dimensions={1}, use_global_device_ids=true | all-gather | bytes 655360 | tf_op jit(solution)/shard_map/all_gather | solution.py:225
  47.7 9.9 all-gather.4.cloned.1.call-done
  57.7 47.1 %all-gather.6.cloned.1.call-done = bf16[1,512,2048]{2,1,0:T(8,128)(2,1)} async-done(((bf16[1,128,2048]{2,1,0:T(8,128)(2,1)}), bf16[1,512,2048]{2,1,0:T(8,128)(2,1)}) %all-gather.6.cloned.1.call-update) | async-done | bytes 2097168 | tf_op jit(solution)/shard_map/all_gather | solution.py:226
  104.8 46.9 %all-gather.8.cloned.1.call-done = bf16[1,2048,512]{2,1,0:T(8,128)(2,1)} async-done(((bf16[1,512,512]{2,1,0:T(8,128)(2,1)}), bf16[1,2048,512]{2,1,0:T(8,128)(2,1)}) %all-gather.8.cloned.1.call-update) | async-done | bytes 2097168 | tf_op jit(solution)/shard_map/all_gather | solution.py:227
  155.7 359.6 %while.51 = (s32[]{:T(128)}, bf16[1,256,512]{2,1,0:T(8,128)(2,1)S(1)}, f32[8,1,256,512]{3,2,1,0:T(8,128)}, bf16[8,1,256,512]{3,2,1,0:T(8,128)(2,1)}, f32[28,512]...) while((s32[]{:T(128)}, ...), condition=%wide.region_15.16_spmd.clone.clone, body=%wide.region_0.15_spmd.clone.clone.sunk | while | flops 1894023424 | bytes 21152720 | solution.py:278
  160.1 19.6 %collective-permute-done.1 = bf16[1,256,512]{2,1,0:T(8,128)(2,1)S(1)} collective-permute-done((bf16[1,256,512]{2,1,0:T(8,128)(2,1)}, bf16[1,256,512]{2,1,0:T(8,128)(2,1)S(1)}, u32[]{:S(2)}, u32[]{:S(2)}) %collective-permute-start.1) | collective-permute-done | bytes 262176 | tf_op jit(solution)/shard_map/while/body/eval_jaxpr/ppermute | solution.py:18
  179.7 20.8 %conditional.8 = (bf16[1,256,512]{2,1,0:T(8,128)(2,1)}, f32[8,1,256,512]{3,2,1,0:T(8,128)}, bf16[8,1,256,512]{3,2,1,0:T(8,128)(2,1)}, f32[28,512]{1,0:T(8,128)S(1)}) conditional(s32[]{:T(128)} %convert_element_type.422, (f32[8,1,256,512]{3,2,1,0:T(8,128)}, bf16[8,1,256,512]{3,2,1,0:T(8,128)(2,1)}, f32[28,512]{1,0:T(8,128)S(1)}) %tuple.128, ...), branch_computations={%region_1.1_spmd, %region_2.14_spmd} | conditional | flops 1894023424 | bytes 20103596 | solution.py:266
  206.0 20.8 %conditional.8 = (bf16[1,256,512]{2,1,0:T(8,128)(2,1)}, f32[8,1,256,512]{3,2,1,0:T(8,128)}, bf16[8,1,256,512]{3,2,1,0:T(8,128)(2,1)}, f32[28,512]{1,0:T(8,128)S(1)}) conditional(s32[]{:T(128)} %convert_element_type.422, (f32[8,1,256,512]{3,2,1,0:T(8,128)}, bf16[8,1,256,512]{3,2,1,0:T(8,128)(2,1)}, f32[28,512]{1,0:T(8,128)S(1)}) %tuple.128, ...), branch_computations={%region_1.1_spmd, %region_2.14_spmd} | conditional | flops 1894023424 | bytes 20103596 | solution.py:266
  234.7 20.7 %conditional.8 = (bf16[1,256,512]{2,1,0:T(8,128)(2,1)}, f32[8,1,256,512]{3,2,1,0:T(8,128)}, bf16[8,1,256,512]{3,2,1,0:T(8,128)(2,1)}, f32[28,512]{1,0:T(8,128)S(1)}) conditional(s32[]{:T(128)} %convert_element_type.422, (f32[8,1,256,512]{3,2,1,0:T(8,128)}, bf16[8,1,256,512]{3,2,1,0:T(8,128)(2,1)}, f32[28,512]{1,0:T(8,128)S(1)}) %tuple.128, ...), branch_computations={%region_1.1_spmd, %region_2.14_spmd} | conditional | flops 1894023424 | bytes 20103596 | solution.py:266
  263.4 20.7 %conditional.8 = (bf16[1,256,512]{2,1,0:T(8,128)(2,1)}, f32[8,1,256,512]{3,2,1,0:T(8,128)}, bf16[8,1,256,512]{3,2,1,0:T(8,128)(2,1)}, f32[28,512]{1,0:T(8,128)S(1)}) conditional(s32[]{:T(128)} %convert_element_type.422, (f32[8,1,256,512]{3,2,1,0:T(8,128)}, bf16[8,1,256,512]{3,2,1,0:T(8,128)(2,1)}, f32[28,512]{1,0:T(8,128)S(1)}) %tuple.128, ...), branch_computations={%region_1.1_spmd, %region_2.14_spmd} | conditional | flops 1894023424 | bytes 20103596 | solution.py:266
  292.0 20.8 %conditional.8 = (bf16[1,256,512]{2,1,0:T(8,128)(2,1)}, f32[8,1,256,512]{3,2,1,0:T(8,128)}, bf16[8,1,256,512]{3,2,1,0:T(8,128)(2,1)}, f32[28,512]{1,0:T(8,128)S(1)}) conditional(s32[]{:T(128)} %convert_element_type.422, (f32[8,1,256,512]{3,2,1,0:T(8,128)}, bf16[8,1,256,512]{3,2,1,0:T(8,128)(2,1)}, f32[28,512]{1,0:T(8,128)S(1)}) %tuple.128, ...), branch_computations={%region_1.1_spmd, %region_2.14_spmd} | conditional | flops 1894023424 | bytes 20103596 | solution.py:266
  320.7 20.7 %conditional.8 = (bf16[1,256,512]{2,1,0:T(8,128)(2,1)}, f32[8,1,256,512]{3,2,1,0:T(8,128)}, bf16[8,1,256,512]{3,2,1,0:T(8,128)(2,1)}, f32[28,512]{1,0:T(8,128)S(1)}) conditional(s32[]{:T(128)} %convert_element_type.422, (f32[8,1,256,512]{3,2,1,0:T(8,128)}, bf16[8,1,256,512]{3,2,1,0:T(8,128)(2,1)}, f32[28,512]{1,0:T(8,128)S(1)}) %tuple.128, ...), branch_computations={%region_1.1_spmd, %region_2.14_spmd} | conditional | flops 1894023424 | bytes 20103596 | solution.py:266
  349.3 20.7 %conditional.8 = (bf16[1,256,512]{2,1,0:T(8,128)(2,1)}, f32[8,1,256,512]{3,2,1,0:T(8,128)}, bf16[8,1,256,512]{3,2,1,0:T(8,128)(2,1)}, f32[28,512]{1,0:T(8,128)S(1)}) conditional(s32[]{:T(128)} %convert_element_type.422, (f32[8,1,256,512]{3,2,1,0:T(8,128)}, bf16[8,1,256,512]{3,2,1,0:T(8,128)(2,1)}, f32[28,512]{1,0:T(8,128)S(1)}) %tuple.128, ...), branch_computations={%region_1.1_spmd, %region_2.14_spmd} | conditional | flops 1894023424 | bytes 20103596 | solution.py:266
  378.0 20.8 %conditional.8 = (bf16[1,256,512]{2,1,0:T(8,128)(2,1)}, f32[8,1,256,512]{3,2,1,0:T(8,128)}, bf16[8,1,256,512]{3,2,1,0:T(8,128)(2,1)}, f32[28,512]{1,0:T(8,128)S(1)}) conditional(s32[]{:T(128)} %convert_element_type.422, (f32[8,1,256,512]{3,2,1,0:T(8,128)}, bf16[8,1,256,512]{3,2,1,0:T(8,128)(2,1)}, f32[28,512]{1,0:T(8,128)S(1)}) %tuple.128, ...), branch_computations={%region_1.1_spmd, %region_2.14_spmd} | conditional | flops 1894023424 | bytes 20103596 | solution.py:266
  407.3 24.3 %collective-permute-start.1 = (bf16[1,256,512]{2,1,0:T(8,128)(2,1)}, bf16[1,256,512]{2,1,0:T(8,128)(2,1)S(1)}, u32[]{:S(2)}, u32[]{:S(2)}) collective-permute-start(bf16[1,256,512]{2,1,0:T(8,128)(2,1)} %get-tuple-element.1488), channel_id=1, source_target_pairs={{0,4},{4,8},{8,12},{12,16},{16,20},{20,24},{24,28},{1,5},{5,9},{9,... | collective-permute-start | bytes 786440 | tf_op jit(solution)/shard_map/while/body/eval_jaxpr/ppermute | solution.py:18
  444.6 18.5 %collective-permute-start.1 = (bf16[1,256,512]{2,1,0:T(8,128)(2,1)}, bf16[1,256,512]{2,1,0:T(8,128)(2,1)S(1)}, u32[]{:S(2)}, u32[]{:S(2)}) collective-permute-start(bf16[1,256,512]{2,1,0:T(8,128)(2,1)} %get-tuple-element.1488), channel_id=1, source_target_pairs={{0,4},{4,8},{8,12},{12,16},{16,20},{20,24},{24,28},{1,5},{5,9},{9,... | collective-permute-start | bytes 786440 | tf_op jit(solution)/shard_map/while/body/eval_jaxpr/ppermute | solution.py:18
  476.9 25.2 %collective-permute-start.1 = (bf16[1,256,512]{2,1,0:T(8,128)(2,1)}, bf16[1,256,512]{2,1,0:T(8,128)(2,1)S(1)}, u32[]{:S(2)}, u32[]{:S(2)}) collective-permute-start(bf16[1,256,512]{2,1,0:T(8,128)(2,1)} %get-tuple-element.1488), channel_id=1, source_target_pairs={{0,4},{4,8},{8,12},{12,16},{16,20},{20,24},{24,28},{1,5},{5,9},{9,... | collective-permute-start | bytes 786440 | tf_op jit(solution)/shard_map/while/body/eval_jaxpr/ppermute | solution.py:18
  524.6 903.8 %while.50 = (s32[]{:T(128)}, bf16[1,256,512]{2,1,0:T(8,128)(2,1)S(1)}, f32[1,2,512]{2,1,0:T(2,128)}, f32[1,2,512]{2,1,0:T(2,128)}, f32[1,512,1536]{2,1,0:T(8,128...) while((s32[]{:T(128)}, ...), condition=%wide.region_34.35_spmd.clone, body=%wide.region_16.34_spmd.clone.sunk | while | flops 4779334656 | bytes 202318640 | solution.py:317
  527.3 16.9 %collective-permute-done = bf16[1,256,512]{2,1,0:T(8,128)(2,1)S(1)} collective-permute-done((bf16[1,256,512]{2,1,0:T(8,128)(2,1)}, bf16[1,256,512]{2,1,0:T(8,128)(2,1)S(1)}, u32[]{:S(2)}, u32[]{:S(2)}) %collective-permute-start) | collective-permute-done | bytes 262176 | tf_op jit(solution)/shard_map/while/body/eval_jaxpr/ppermute | solution.py:18
  546.8 6.7 collective-permute-done
  556.2 23.4 %collective-permute-done = bf16[1,256,512]{2,1,0:T(8,128)(2,1)S(1)} collective-permute-done((bf16[1,256,512]{2,1,0:T(8,128)(2,1)}, bf16[1,256,512]{2,1,0:T(8,128)(2,1)S(1)}, u32[]{:S(2)}, u32[]{:S(2)}) %collective-permute-start) | collective-permute-done | bytes 262176 | tf_op jit(solution)/shard_map/while/body/eval_jaxpr/ppermute | solution.py:18
  582.2 6.9 collective-permute-done
  591.7 16.7 %collective-permute-done = bf16[1,256,512]{2,1,0:T(8,128)(2,1)S(1)} collective-permute-done((bf16[1,256,512]{2,1,0:T(8,128)(2,1)}, bf16[1,256,512]{2,1,0:T(8,128)(2,1)S(1)}, u32[]{:S(2)}, u32[]{:S(2)}) %collective-permute-start) | collective-permute-done | bytes 262176 | tf_op jit(solution)/shard_map/while/body/eval_jaxpr/ppermute | solution.py:18
  611.1 297.7 %collective-permute-done = bf16[1,256,512]{2,1,0:T(8,128)(2,1)S(1)} collective-permute-done((bf16[1,256,512]{2,1,0:T(8,128)(2,1)}, bf16[1,256,512]{2,1,0:T(8,128)(2,1)S(1)}, u32[]{:S(2)}, u32[]{:S(2)}) %collective-permute-start) | collective-permute-done | bytes 262176 | tf_op jit(solution)/shard_map/while/body/eval_jaxpr/ppermute | solution.py:18
  908.8 50.2 %conditional.7 = (bf16[1,256,512]{2,1,0:T(8,128)(2,1)}, f32[1,2,512]{2,1,0:T(2,128)}, f32[1,2,512]{2,1,0:T(2,128)}, f32[1,512,1536]{2,1,0:T(8,128)}, f32[1,512,5...) conditional(s32[]{:T(128)} %convert_element_type.421, ...), branch_computations={%region_17.17_spmd, %region_18.33_spmd} | conditional | flops 4779334656 | bytes 201269424 | solution.py:311
  960.9 6.8 collective-permute-done
  967.7 50.2 %conditional.7 = (bf16[1,256,512]{2,1,0:T(8,128)(2,1)}, f32[1,2,512]{2,1,0:T(2,128)}, f32[1,2,512]{2,1,0:T(2,128)}, f32[1,512,1536]{2,1,0:T(8,128)}, f32[1,512,5...) conditional(s32[]{:T(128)} %convert_element_type.421, ...), branch_computations={%region_17.17_spmd, %region_18.33_spmd} | conditional | flops 4779334656 | bytes 201269424 | solution.py:311
  1019.8 6.9 collective-permute-done
  1026.6 50.2 %conditional.7 = (bf16[1,256,512]{2,1,0:T(8,128)(2,1)}, f32[1,2,512]{2,1,0:T(2,128)}, f32[1,2,512]{2,1,0:T(2,128)}, f32[1,512,1536]{2,1,0:T(8,128)}, f32[1,512,5...) conditional(s32[]{:T(128)} %convert_element_type.421, ...), branch_computations={%region_17.17_spmd, %region_18.33_spmd} | conditional | flops 4779334656 | bytes 201269424 | solution.py:311
  1078.7 6.9 collective-permute-done
  1085.5 50.2 %conditional.7 = (bf16[1,256,512]{2,1,0:T(8,128)(2,1)}, f32[1,2,512]{2,1,0:T(2,128)}, f32[1,2,512]{2,1,0:T(2,128)}, f32[1,512,1536]{2,1,0:T(8,128)}, f32[1,512,5...) conditional(s32[]{:T(128)} %convert_element_type.421, ...), branch_computations={%region_17.17_spmd, %region_18.33_spmd} | conditional | flops 4779334656 | bytes 201269424 | solution.py:311
  1137.6 6.9 collective-permute-done
  1144.5 50.2 %conditional.7 = (bf16[1,256,512]{2,1,0:T(8,128)(2,1)}, f32[1,2,512]{2,1,0:T(2,128)}, f32[1,2,512]{2,1,0:T(2,128)}, f32[1,512,1536]{2,1,0:T(8,128)}, f32[1,512,5...) conditional(s32[]{:T(128)} %convert_element_type.421, ...), branch_computations={%region_17.17_spmd, %region_18.33_spmd} | conditional | flops 4779334656 | bytes 201269424 | solution.py:311
  1196.5 6.9 collective-permute-done
  1203.4 50.2 %conditional.7 = (bf16[1,256,512]{2,1,0:T(8,128)(2,1)}, f32[1,2,512]{2,1,0:T(2,128)}, f32[1,2,512]{2,1,0:T(2,128)}, f32[1,512,1536]{2,1,0:T(8,128)}, f32[1,512,5...) conditional(s32[]{:T(128)} %convert_element_type.421, ...), branch_computations={%region_17.17_spmd, %region_18.33_spmd} | conditional | flops 4779334656 | bytes 201269424 | solution.py:311
  1255.5 6.9 collective-permute-done
  1262.3 50.2 %conditional.7 = (bf16[1,256,512]{2,1,0:T(8,128)(2,1)}, f32[1,2,512]{2,1,0:T(2,128)}, f32[1,2,512]{2,1,0:T(2,128)}, f32[1,512,1536]{2,1,0:T(8,128)}, f32[1,512,5...) conditional(s32[]{:T(128)} %convert_element_type.421, ...), branch_computations={%region_17.17_spmd, %region_18.33_spmd} | conditional | flops 4779334656 | bytes 201269424 | solution.py:311
  1314.4 6.9 collective-permute-done
  1321.3 50.2 %conditional.7 = (bf16[1,256,512]{2,1,0:T(8,128)(2,1)}, f32[1,2,512]{2,1,0:T(2,128)}, f32[1,2,512]{2,1,0:T(2,128)}, f32[1,512,1536]{2,1,0:T(8,128)}, f32[1,512,5...) conditional(s32[]{:T(128)} %convert_element_type.421, ...), branch_computations={%region_17.17_spmd, %region_18.33_spmd} | conditional | flops 4779334656 | bytes 201269424 | solution.py:311
  1380.0 47.0 %collective-permute-start = (bf16[1,256,512]{2,1,0:T(8,128)(2,1)}, bf16[1,256,512]{2,1,0:T(8,128)(2,1)S(1)}, u32[]{:S(2)}, u32[]{:S(2)}) collective-permute-start(bf16[1,256,512]{2,1,0:T(8,128)(2,1)} %get-tuple-element.1463), channel_id=1, source_target_pairs={{4,0},{8,4},{12,8},{16,12},{20,16},{24,20},{28,24},{5,1},{9,5},{13... | collective-permute-start | bytes 786440 | tf_op jit(solution)/shard_map/while/body/eval_jaxpr/ppermute | solution.py:18
  1447.4 16.4 reduce-scatter.24.cloned.1.call-done
  1465.3 35.4 %reduce-scatter.22.cloned.1.call-done = bf16[64,28]{1,0:T(8,128)(2,1)} async-done(((bf16[512,28]{1,0:T(8,128)(2,1)}), bf16[64,28]{1,0:T(8,128)(2,1)}) %reduce-scatter.22.cloned.1.call-update) | async-done | bytes 3600
  1501.5 16.3 psum.7
  1517.7 6.0 reduce-scatter.16.cloned.1.call-done
  1525.4 36.2 %reduce-scatter.14.cloned.1.call-done = bf16[1,128,1536]{2,1,0:T(8,128)(2,1)} async-done(((bf16[1,512,1536]{2,1,0:T(8,128)(2,1)}), bf16[1,128,1536]{2,1,0:T(8,128)(2,1)}) %reduce-scatter.14.cloned.1.call-update) | async-done | bytes 393232 | tf_op jit(solution)/shard_map/reduce_scatter | solution.py:326
  1563.5 43.3 %reduce-scatter.20.cloned.1.call-done = bf16[1,512,512]{2,1,0:T(8,128)(2,1)} async-done(((bf16[1,2048,512]{2,1,0:T(8,128)(2,1)}), bf16[1,512,512]{2,1,0:T(8,128)(2,1)}) %reduce-scatter.20.cloned.1.call-update) | async-done | bytes 524304 | tf_op jit(solution)/shard_map/reduce_scatter | solution.py:335
  1609.0 43.2 %reduce-scatter.18.cloned.1.call-done = bf16[1,128,2048]{2,1,0:T(8,128)(2,1)} async-done(((bf16[1,512,2048]{2,1,0:T(8,128)(2,1)}), bf16[1,128,2048]{2,1,0:T(8,128)(2,1)}) %reduce-scatter.18.cloned.1.call-update) | async-done | bytes 524304 | tf_op jit(solution)/shard_map/reduce_scatter | solution.py:332
  (1349 shorter events, 770.7 us)
Async XLA Ops:
  7.2 50.5 %all-gather.4.cloned.1.call-start = ((), (), s32[]{:S(2)}) async-start(), calls=%async_computation.7 | async-start | bytes 1966080 | tf_op jit(solution)/shard_map/all_gather | solution.py:224
  9.4 95.4 %all-gather.6.cloned.1.call-start = ((), (), s32[]{:S(2)}) async-start(), calls=%async_computation.8 | async-start | bytes 2621440 | tf_op jit(solution)/shard_map/all_gather | solution.py:226
  10.3 36.7 %copy-start.44 = (s32[8,1]{0,1:T(1,128)S(1)}, s32[8,1]{0,1:T(1,128)}, u32[]{:S(2)}) copy-start(s32[8,1]{0,1:T(1,128)} %param.20) | copy-start | bytes 100
  10.3 36.7 %copy-start.40 = (s32[8,1,256]{2,1,0:T(1,128)S(1)}, s32[8,1,256]{2,1,0:T(1,128)}, u32[]{:S(2)}) copy-start(s32[8,1,256]{2,1,0:T(1,128)} %param.19) | copy-start | bytes 24580
  10.3 36.8 %copy-start.41 = (s32[8,1,256]{2,1,0:T(1,128)S(1)}, s32[8,1,256]{2,1,0:T(1,128)}, u32[]{:S(2)}) copy-start(s32[8,1,256]{2,1,0:T(1,128)} %param.18) | copy-start | bytes 24580
  10.3 141.3 %all-gather.8.cloned.1.call-start = ((), (), s32[]{:S(2)}) async-start(), calls=%async_computation.9 | async-start | bytes 2621440 | tf_op jit(solution)/shard_map/all_gather | solution.py:227
  11.3 1434.7 %reduce-scatter.26.cloned.1.call-start = ((), (), s32[]{:S(2)}) async-start(), calls=%async_computation.16 | async-start | bytes 163840
  156.5 23.2 %collective-permute-start.1 = (bf16[1,256,512]{2,1,0:T(8,128)(2,1)}, bf16[1,256,512]{2,1,0:T(8,128)(2,1)S(1)}, u32[]{:S(2)}, u32[]{:S(2)}) collective-permute-start(bf16[1,256,512]{2,1,0:T(8,128)(2,1)} %get-tuple-element.1488), channel_id=1, source_target_pairs={{0,4},{4,8},{8,12},{12,16},{16,20},{20,24},{24,28},{1,5},{5,9},{9,... | collective-permute-start | bytes 786440 | tf_op jit(solution)/shard_map/while/body/eval_jaxpr/ppermute | solution.py:18
  200.5 5.5 collective-permute-start.1
  226.8 7.9 collective-permute-start.1
  255.4 8.0 collective-permute-start.1
  284.1 7.9 collective-permute-start.1
  312.8 7.9 collective-permute-start.1
  341.4 7.9 collective-permute-start.1
  370.1 7.9 collective-permute-start.1
  398.7 7.9 collective-permute-start.1
  407.3 27.9 %collective-permute-start.1 = (bf16[1,256,512]{2,1,0:T(8,128)(2,1)}, bf16[1,256,512]{2,1,0:T(8,128)(2,1)S(1)}, u32[]{:S(2)}, u32[]{:S(2)}) collective-permute-start(bf16[1,256,512]{2,1,0:T(8,128)(2,1)} %get-tuple-element.1488), channel_id=1, source_target_pairs={{0,4},{4,8},{8,12},{12,16},{16,20},{20,24},{24,28},{1,5},{5,9},{9,... | collective-permute-start | bytes 786440 | tf_op jit(solution)/shard_map/while/body/eval_jaxpr/ppermute | solution.py:18
  436.0 7.9 collective-permute-start.1
  444.6 22.2 %collective-permute-start.1 = (bf16[1,256,512]{2,1,0:T(8,128)(2,1)}, bf16[1,256,512]{2,1,0:T(8,128)(2,1)S(1)}, u32[]{:S(2)}, u32[]{:S(2)}) collective-permute-start(bf16[1,256,512]{2,1,0:T(8,128)(2,1)} %get-tuple-element.1488), channel_id=1, source_target_pairs={{0,4},{4,8},{8,12},{12,16},{16,20},{20,24},{24,28},{1,5},{5,9},{9,... | collective-permute-start | bytes 786440 | tf_op jit(solution)/shard_map/while/body/eval_jaxpr/ppermute | solution.py:18
  467.5 8.8 collective-permute-start.1
  476.9 28.8 %collective-permute-start.1 = (bf16[1,256,512]{2,1,0:T(8,128)(2,1)}, bf16[1,256,512]{2,1,0:T(8,128)(2,1)S(1)}, u32[]{:S(2)}, u32[]{:S(2)}) collective-permute-start(bf16[1,256,512]{2,1,0:T(8,128)(2,1)} %get-tuple-element.1488), channel_id=1, source_target_pairs={{0,4},{4,8},{8,12},{12,16},{16,20},{20,24},{24,28},{1,5},{5,9},{9,... | collective-permute-start | bytes 786440 | tf_op jit(solution)/shard_map/while/body/eval_jaxpr/ppermute | solution.py:18
  506.5 8.8 collective-permute-start.1
  524.6 907.1 %copy-start.16 = (f32[28,512]{1,0:T(8,128)S(1)}, f32[28,512]{1,0:T(8,128)}, u32[]{:S(2)}) copy-start(f32[28,512]{1,0:T(8,128)} %copy-done.15) | copy-start | bytes 172036
  525.4 18.8 %collective-permute-start = (bf16[1,256,512]{2,1,0:T(8,128)(2,1)}, bf16[1,256,512]{2,1,0:T(8,128)(2,1)S(1)}, u32[]{:S(2)}, u32[]{:S(2)}) collective-permute-start(bf16[1,256,512]{2,1,0:T(8,128)(2,1)} %get-tuple-element.1463), channel_id=1, source_target_pairs={{4,0},{8,4},{12,8},{16,12},{20,16},{24,20},{28,24},{5,1},{9,5},{13... | collective-permute-start | bytes 786440 | tf_op jit(solution)/shard_map/while/body/eval_jaxpr/ppermute | solution.py:18
  544.9 8.7 collective-permute-start
  554.3 25.3 %collective-permute-start = (bf16[1,256,512]{2,1,0:T(8,128)(2,1)}, bf16[1,256,512]{2,1,0:T(8,128)(2,1)S(1)}, u32[]{:S(2)}, u32[]{:S(2)}) collective-permute-start(bf16[1,256,512]{2,1,0:T(8,128)(2,1)} %get-tuple-element.1463), channel_id=1, source_target_pairs={{4,0},{8,4},{12,8},{16,12},{20,16},{24,20},{28,24},{5,1},{9,5},{13... | collective-permute-start | bytes 786440 | tf_op jit(solution)/shard_map/while/body/eval_jaxpr/ppermute | solution.py:18
  580.3 8.8 collective-permute-start
  589.8 18.7 %collective-permute-start = (bf16[1,256,512]{2,1,0:T(8,128)(2,1)}, bf16[1,256,512]{2,1,0:T(8,128)(2,1)S(1)}, u32[]{:S(2)}, u32[]{:S(2)}) collective-permute-start(bf16[1,256,512]{2,1,0:T(8,128)(2,1)} %get-tuple-element.1463), channel_id=1, source_target_pairs={{4,0},{8,4},{12,8},{16,12},{20,16},{24,20},{28,24},{5,1},{9,5},{13... | collective-permute-start | bytes 786440 | tf_op jit(solution)/shard_map/while/body/eval_jaxpr/ppermute | solution.py:18
  609.2 299.6 %collective-permute-start = (bf16[1,256,512]{2,1,0:T(8,128)(2,1)}, bf16[1,256,512]{2,1,0:T(8,128)(2,1)S(1)}, u32[]{:S(2)}, u32[]{:S(2)}) collective-permute-start(bf16[1,256,512]{2,1,0:T(8,128)(2,1)} %get-tuple-element.1463), channel_id=1, source_target_pairs={{4,0},{8,4},{12,8},{16,12},{20,16},{24,20},{28,24},{5,1},{9,5},{13... | collective-permute-start | bytes 786440 | tf_op jit(solution)/shard_map/while/body/eval_jaxpr/ppermute | solution.py:18
  959.0 8.7 collective-permute-start
  972.6 7.7 copy-start.20
  1017.8 8.8 collective-permute-start
  1031.6 7.7 copy-start.20
  1076.8 8.8 collective-permute-start
  1090.5 7.7 copy-start.20
  1135.7 8.8 collective-permute-start
  1149.4 7.7 copy-start.20
  1194.6 8.8 collective-permute-start
  1253.6 8.8 collective-permute-start
  1312.5 8.8 collective-permute-start
  1371.4 7.9 collective-permute-start
  1380.0 48.4 %collective-permute-start = (bf16[1,256,512]{2,1,0:T(8,128)(2,1)}, bf16[1,256,512]{2,1,0:T(8,128)(2,1)S(1)}, u32[]{:S(2)}, u32[]{:S(2)}) collective-permute-start(bf16[1,256,512]{2,1,0:T(8,128)(2,1)} %get-tuple-element.1463), channel_id=1, source_target_pairs={{4,0},{8,4},{12,8},{16,12},{20,16},{24,20},{28,24},{5,1},{9,5},{13... | collective-permute-start | bytes 786440 | tf_op jit(solution)/shard_map/while/body/eval_jaxpr/ppermute | solution.py:18
  1430.1 33.8 %reduce-scatter.24.cloned.1.call-start = ((), (), s32[]{:S(2)}) async-start(), calls=%async_computation.15 | async-start | bytes 163840
  1431.7 69.0 %reduce-scatter.22.cloned.1.call-start = ((), (), s32[]{:S(2)}) async-start(), calls=%async_computation.14 | async-start | bytes 147456
  1432.6 91.2 %reduce-scatter.16.cloned.1.call-start = ((), (), s32[]{:S(2)}) async-start(), calls=%async_computation.11 | async-start | bytes 655360 | tf_op jit(solution)/shard_map/reduce_scatter | solution.py:329
  1434.8 126.8 %reduce-scatter.14.cloned.1.call-start = ((), (), s32[]{:S(2)}) async-start(), calls=%async_computation.10 | async-start | bytes 1966080 | tf_op jit(solution)/shard_map/reduce_scatter | solution.py:326
  1438.0 168.8 %reduce-scatter.20.cloned.1.call-start = ((), (), s32[]{:S(2)}) async-start(), calls=%async_computation.13 | async-start | bytes 2621440 | tf_op jit(solution)/shard_map/reduce_scatter | solution.py:335
  1442.0 210.2 %reduce-scatter.18.cloned.1.call-start = ((), (), s32[]{:S(2)}) async-start(), calls=%async_computation.12 | async-start | bytes 2621440 | tf_op jit(solution)/shard_map/reduce_scatter | solution.py:332
  (299 other events, 878.7 us)
Sparse Core Ops, SparseCore 0:
  10.2 47.4 all-gather.3
  59.8 44.9 all-gather.5
  106.9 44.6 all-gather.7
  1430.2 13.4 reduce-scatter.25
  1446.4 17.3 reduce-scatter.23
  1467.3 33.3 reduce-scatter.21
  1503.6 20.1 reduce-scatter.15
  1526.2 35.3 reduce-scatter.13
  1564.0 42.8 reduce-scatter.19
  1609.0 43.1 reduce-scatter.17
where the time goes:
time: 1670 us; the launch traced here: 1660 us
  waiting for transfers between devices  778 us (47%)
  matrix products  349 us (21%)
  starting transfers between devices  192 us (11%)
  other arithmetic  150 us (9%)
  local copies, waits for them, and re-layouts  120 us (7%)
  blocking collectives  51.8 us (3%)
    ppermute x30, waiting for transfers between devices, shifted_2(): return lax.ppermute(block, axis, route)  494 us
    ppermute x30, starting transfers between devices, shifted_2(): return lax.ppermute(block, axis, route)  192 us
    dot_general x48, matrix products, matmul_rows(): jnp.einsum('btd,de->bte', left, right, preferred_element_type=jnp.float32)  116 us
    dot_general x24, matrix products, outer_sum(): jnp.einsum('btd,bte->de', left, gradient, preferred_element_type=jnp.floa...  68.2 us
    dot_general x24, matrix products, matmul_back(): jnp.einsum('bte,de->btd', gradient, right, preferred_element_type=jnp.flo...  62.3 us
    unnamed x13, waiting for transfers between devices  52 us
    cond x592, local copies, waits for them, and re-layouts  50.8 us
    all_gather x1, waiting for transfers between devices, body(): lax.all_gather(w_in.astype(jnp.bfloat16), 'dp', axis=1, tiled=True)  47.1 us
  transfers between devices with their start and end apart: 40, of which 39 were waited for; matrix products, arithmetic and copies ran while one was open for 2% of the time, Pallas kernels for 0%

commit v1 on v0

v1 whole, which is shorter than its diff:
```python
import functools
import math

import jax
import jax.numpy as jnp
from jax import lax
from jax.experimental import pallas as pl
from jax.experimental.pallas import tpu as pltpu
from jax.sharding import PartitionSpec as P

HEADS = 8
EPSILON = 1e-05
EMBED_GAIN = 16.0
FF_CHUNK = 512
MESH = pl.DeviceIdType.MESH


def dot(left, right, left_dim, right_dim):
    return lax.dot_general(
        left, right, (((left_dim,), (right_dim,)), ((), ())), preferred_element_type=jnp.float32
    )


def unit_rows(values):
    average = jnp.mean(values, axis=-1, keepdims=True)
    centered = values - average
    variance = jnp.mean(centered * centered, axis=-1, keepdims=True)
    scale = lax.rsqrt(variance + EPSILON)
    return centered * scale, scale


def unit_back(gradient, unit, scale):
    first = jnp.mean(gradient, axis=-1, keepdims=True)
    second = jnp.mean(gradient * unit, axis=-1, keepdims=True)
    return scale * (gradient - first - unit * second)


def fold_rows(values):
    rows, columns = values.shape
    return jnp.sum(values.reshape(rows // 8, 8, columns), axis=0)


def pipeline_kernel(
    stages,
    token_ref,
    order_ref,
    stamp_ref,
    table_ref,
    gain_ref,
    bias_ref,
    w_qkv_ref,
    w_out_ref,
    w_in_ref,
    w_down_ref,
    d_table_ref,
    d_gain_ref,
    d_bias_ref,
    d_qkv_ref,
    d_out_ref,
    d_in_ref,
    d_down_ref,
    stash_ref,
    h_in,
    g_in,
    h_send,
    g_send,
    packed,
    mixed,
    middle,
    active,
    slope,
    attention_out,
    attention_in,
    work,
    table_parts,
    norm_sums,
    table_sum,
    h_send_sem,
    h_recv_sem,
    g_send_sem,
    g_recv_sem,
    stash_sem,
):
    micro_count, _, length = token_ref.shape
    vocab, width = table_ref.shape
    hidden_units = w_in_ref.shape[1]
    head_size = width // HEADS
    score_scale = 1.0 / math.sqrt(head_size)
    pair_width = 2 * head_size
    stage = lax.axis_index("section")
    last = stages - 1
    bf16, f32 = jnp.bfloat16, jnp.float32

    if stages > 1:
        ahead, behind = lax.rem(stage + 1, stages), lax.rem(stage + stages - 1, stages)
        barrier = pltpu.get_barrier_semaphore()
        for neighbour in (ahead, behind):
            pl.semaphore_signal(
                barrier, inc=1, device_id={"section": neighbour}, device_id_type=MESH
            )
        pl.semaphore_wait(barrier, 2)

    table_rows = table_parts.shape[1]
    work[:table_rows, :] = jnp.zeros((table_rows, width), f32)
    work[:vocab, :] = table_ref[...]
    rest = work[:table_rows, :]
    for part in range(3):
        rounded = rest.astype(bf16)
        table_parts[part] = rounded
        rest = rest - rounded.astype(f32)
    d_qkv_ref[...] = jnp.zeros_like(d_qkv_ref)
    d_out_ref[...] = jnp.zeros_like(d_out_ref)
    d_in_ref[...] = jnp.zeros_like(d_in_ref)
    d_down_ref[...] = jnp.zeros_like(d_down_ref)
    norm_sums[...] = jnp.zeros_like(norm_sums)
    table_sum[...] = jnp.zeros_like(table_sum)

    letters = lax.broadcasted_iota(jnp.int32, (table_rows, length), 0)
    lane = lax.broadcasted_iota(jnp.int32, (length, pair_width), 1)
    lower = lane < head_size

    def shown_rows(micro):
        visible = order_ref[micro] < stamp_ref[micro]
        shown = jnp.where(visible, token_ref[micro], vocab - 1)
        return (letters == shown).astype(bf16)

    def halves(pair):
        zero = jnp.zeros_like(pair)
        return jnp.where(lower, pair, zero), jnp.where(lower, zero, pair)

    def load_hidden(micro):
        @pl.when(stage == 0)
        def _():
            hot = shown_rows(micro)
            total = dot(hot, table_parts[2], 0, 0)
            total = total + dot(hot, table_parts[1], 0, 0)
            total = total + dot(hot, table_parts[0], 0, 0)
            work[...] = total * EMBED_GAIN

        @pl.when(stage > 0)
        def _():
            work[...] = h_in[micro].astype(f32)

    def hidden_copy(micro, target):
        slot = lax.rem(micro, 2)
        return pltpu.make_async_remote_copy(
            src_ref=h_send.at[slot],
            dst_ref=h_in.at[micro],
            send_sem=h_send_sem.at[slot],
            recv_sem=h_recv_sem.at[micro],
            device_id={"section": target},
            device_id_type=MESH,
        )

    def gradient_copy(micro, target):
        slot = lax.rem(micro, 2)
        return pltpu.make_async_remote_copy(
            src_ref=g_send.at[slot],
            dst_ref=g_in.at[micro],
            send_sem=g_send_sem.at[slot],
            recv_sem=g_recv_sem.at[micro],
            device_id={"section": target},
            device_id_type=MESH,
        )

    def forward(micro):
        if stages > 1:
            @pl.when(stage > 0)
            def _():
                hidden_copy(micro, behind).wait_recv()
        load_hidden(micro)
        hidden = work[...]
        unit, _ = unit_rows(hidden)
        normed = (unit * gain_ref[0:1, :] + bias_ref[0:1, :]).astype(bf16)
        packed[micro] = dot(normed, w_qkv_ref[...], 1, 0).astype(bf16)
        for pair in range(HEADS // 2):
            at = pair * pair_width
            query = packed[micro, :, at : at + pair_width] * jnp.asarray(score_scale, bf16)
            key = packed[micro, :, width + at : width + at + pair_width]
            value = packed[micro, :, 2 * width + at : 2 * width + at + pair_width]
            found = []
            for side, part in enumerate(halves(query)):
                scores = dot(part, key, 1, 1)
                largest = jnp.max(scores, axis=-1, keepdims=True)
                powers = jnp.exp(scores - largest)
                total = jnp.sum(powers, axis=-1, keepdims=True)
                attention = (powers * (1.0 / total)).astype(bf16)
                attention_out[2 * pair + side] = attention
                found.append(dot(attention, value, 1, 0))
            mixed[micro, :, at : at + pair_width] = jnp.where(lower, found[0], found[1]).astype(
                bf16
            )
        save = pltpu.make_async_copy(attention_out, stash_ref.at[micro], stash_sem)
        save.start()
        between = hidden + dot(mixed[micro], w_out_ref[...], 1, 0)
        high = between.astype(bf16)
        middle[micro, 0] = high
        middle[micro, 1] = (between - high.astype(f32)).astype(bf16)
        work[...] = between
        unit, _ = unit_rows(between)
        normed_two = (unit * gain_ref[1:2, :] + bias_ref[1:2, :]).astype(bf16)
        for at in range(0, hidden_units, FF_CHUNK):
            lifted = dot(normed_two, w_in_ref[:, at : at + FF_CHUNK], 1, 0)
            square = lifted * lifted
            inner = math.sqrt(2.0 / math.pi) * lifted * (1.0 + 0.044715 * square)
            bend = jnp.tanh(inner)
            half = 0.5 * (1.0 + bend)
            active[micro, :, at : at + FF_CHUNK] = (lifted * half).astype(bf16)
            steep = math.sqrt(2.0 / math.pi) * (1.0 + 3.0 * 0.044715 * square)
            slope[micro, :, at : at + FF_CHUNK] = (
                half + 0.5 * lifted * (1.0 - bend * bend) * steep
            ).astype(bf16)
        if stages > 1:
            @pl.when(jnp.logical_and(micro >= 2, stage < last))
            def _():
                hidden_copy(micro - 2, ahead).wait_send()
        slot = lax.rem(micro, 2)
        h_send[slot] = (work[...] + dot(active[micro], w_down_ref[...], 1, 0)).astype(bf16)
        if stages > 1:
            @pl.when(stage < last)
            def _():
                hidden_copy(micro, ahead).start()
        save.wait()

    def head(micro):
        unit, scale = unit_rows(h_send[lax.rem(micro, 2)].astype(f32))
        rounded = unit.astype(bf16)
        logits = dot(table_parts[0], rounded, 1, 1)
        logits = jnp.where(letters < vocab, logits, -jnp.inf)
        largest = jnp.max(logits, axis=0, keepdims=True)
        powers = jnp.exp(logits - largest)
        total = jnp.sum(powers, axis=0, keepdims=True)
        stamp = stamp_ref[micro]
        weight = jnp.where(
            order_ref[micro] < stamp, 0.0, 1.0 / (length - stamp).astype(f32)
        )
        target = (letters == token_ref[micro]).astype(f32)
        g_logits = (weight * (powers / total - target)).astype(bf16)
        table_sum[...] += dot(g_logits, rounded, 1, 0)
        g_unit = dot(g_logits, table_parts[0], 0, 0)
        g_in[micro] = unit_back(g_unit, unit, scale).astype(bf16)

    def backward(micro):
        @pl.when(stage == last)
        def _():
            head(micro)

        if stages > 1:
            @pl.when(stage < last)
            def _():
                gradient_copy(micro, ahead).wait_recv()
        load = pltpu.make_async_copy(stash_ref.at[micro], attention_in, stash_sem)
        load.start()
        g_out = g_in[micro]
        for at in range(0, hidden_units, FF_CHUNK):
            g_active = dot(g_out, w_down_ref[at : at + FF_CHUNK, :], 1, 1)
            slope[micro, :, at : at + FF_CHUNK] = (
                g_active * slope[micro, :, at : at + FF_CHUNK].astype(f32)
            ).astype(bf16)
        g_normed = dot(slope[micro], w_in_ref[...], 1, 1)
        unit, scale = unit_rows(middle[micro, 0].astype(f32) + middle[micro, 1].astype(f32))
        middle[micro, 0] = (unit * gain_ref[1:2, :] + bias_ref[1:2, :]).astype(bf16)
        norm_sums[1] += fold_rows(g_normed * unit)
        norm_sums[3] += fold_rows(g_normed)
        g_middle = g_out.astype(f32) + unit_back(g_normed * gain_ref[1:2, :], unit, scale)
        g_attended = g_middle.astype(bf16)
        middle[micro, 1] = g_attended
        g_mixed = dot(g_attended, w_out_ref[...], 1, 1).astype(bf16)
        load_hidden(micro)
        load.wait()
        for pair in range(HEADS // 2):
            at = pair * pair_width
            query = packed[micro, :, at : at + pair_width]
            key = packed[micro, :, width + at : width + at + pair_width]
            value = packed[micro, :, 2 * width + at : 2 * width + at + pair_width]
            g_pair = g_mixed[:, at : at + pair_width]
            found = []
            for side, part in enumerate(halves(g_pair)):
                low = attention_in[2 * pair + side]
                attention = low.astype(f32)
                g_attention = dot(part, value, 1, 1)
                inner = jnp.sum(attention * g_attention, axis=-1, keepdims=True)
                g_scores = (attention * (g_attention - inner)).astype(bf16)
                found.append(
                    (
                        dot(g_scores, key, 1, 0),
                        dot(g_scores, query, 0, 0),
                        dot(low, g_pair, 0, 0),
                    )
                )
            for member, factor in enumerate((score_scale, score_scale, None)):
                joined = jnp.where(lower, found[0][member], found[1][member])
                if factor is not None:
                    joined = joined * factor
                packed[
                    micro, :, member * width + at : member * width + at + pair_width
                ] = joined.astype(bf16)
        g_normed = dot(packed[micro], w_qkv_ref[...], 1, 1)
        unit, scale = unit_rows(work[...])
        h_in[micro] = (unit * gain_ref[0:1, :] + bias_ref[0:1, :]).astype(bf16)
        norm_sums[0] += fold_rows(g_normed * unit)
        norm_sums[2] += fold_rows(g_normed)
        g_hidden = g_middle + unit_back(g_normed * gain_ref[0:1, :], unit, scale)

        @pl.when(stage == 0)
        def _():
            hot = shown_rows(micro)
            high = g_hidden.astype(bf16)
            low = (g_hidden - high.astype(f32)).astype(bf16)
            table_sum[...] += EMBED_GAIN * (dot(hot, high, 1, 0) + dot(hot, low, 1, 0))

        if stages > 1:
            @pl.when(stage > 0)
            def _():
                @pl.when(micro >= 2)
                def _():
                    gradient_copy(micro - 2, behind).wait_send()

                g_send[lax.rem(micro, 2)] = g_hidden.astype(bf16)
                gradient_copy(micro, behind).start()

    def weights(micro):
        d_down_ref[...] += dot(active[micro], g_in[micro], 0, 0)
        d_in_ref[...] += dot(middle[micro, 0], slope[micro], 0, 0)
        d_out_ref[...] += dot(mixed[micro], middle[micro, 1], 0, 0)
        d_qkv_ref[...] += dot(h_in[micro], packed[micro], 0, 0)

    steps = max(2 * last + micro_count, last + 2 * micro_count)

    def step(index, carry):
        f_micro = index - stage
        b_micro = index - (2 * last - stage)
        w_micro = index - jnp.maximum(stage + micro_count, 2 * last - stage)

        @pl.when(jnp.logical_and(f_micro >= 0, f_micro < micro_count))
        def _():
            forward(f_micro)

        @pl.when(jnp.logical_and(b_micro >= 0, b_micro < micro_count))
        def _():
            backward(b_micro)

        @pl.when(jnp.logical_and(w_micro >= 0, w_micro < micro_count))
        def _():
            weights(w_micro)

        return carry

    lax.fori_loop(0, steps, step, 0)

    if stages > 1:
        for micro in range(max(micro_count - 2, 0), micro_count):
            @pl.when(stage < last)
            def _():
                hidden_copy(micro, ahead).wait_send()

            @pl.when(stage > 0)
            def _():
                gradient_copy(micro, behind).wait_send()

    d_table_ref[...] = table_sum[...]
    for member in range(2):
        d_gain_ref[member : member + 1, :] = jnp.sum(norm_sums[member], axis=0, keepdims=True)
        d_bias_ref[member : member + 1, :] = jnp.sum(norm_sums[2 + member], axis=0, keepdims=True)


def run_pipeline(stages, token_ids, order, timesteps, table, gathered):
    gain, bias, w_qkv, w_out, w_in, w_down = gathered
    micro_count, _, length = token_ids.shape
    width = table.shape[1]
    hidden_units = w_in.shape[1]
    rows = -(-table.shape[0] // 32) * 32
    bf16, f32 = jnp.bfloat16, jnp.float32
    vmem = pl.BlockSpec(memory_space=pltpu.VMEM)
    outs = (
        jax.ShapeDtypeStruct((rows, width), f32),
        jax.ShapeDtypeStruct((2, width), f32),
        jax.ShapeDtypeStruct((2, width), f32),
        jax.ShapeDtypeStruct(w_qkv.shape, f32),
        jax.ShapeDtypeStruct(w_out.shape, f32),
        jax.ShapeDtypeStruct(w_in.shape, f32),
        jax.ShapeDtypeStruct(w_down.shape, f32),
        jax.ShapeDtypeStruct((micro_count, HEADS, length, length), bf16),
    )
    rows_shape = (micro_count, length, width)
    return pl.pallas_call(
        functools.partial(pipeline_kernel, stages),
        out_shape=outs,
        in_specs=[vmem] * 10,
        out_specs=[vmem] * 7 + [pl.BlockSpec(memory_space=pl.ANY)],
        scratch_shapes=[
            pltpu.VMEM(rows_shape, bf16),
            pltpu.VMEM(rows_shape, bf16),
            pltpu.VMEM((2, length, width), bf16),
            pltpu.VMEM((2, length, width), bf16),
            pltpu.VMEM((micro_count, length, 3 * width), bf16),
            pltpu.VMEM(rows_shape, bf16),
            pltpu.VMEM((micro_count, 2, length, width), bf16),
            pltpu.VMEM((micro_count, length, hidden_units), bf16),
            pltpu.VMEM((micro_count, length, hidden_units), bf16),
            pltpu.VMEM((HEADS, length, length), bf16),
            pltpu.VMEM((HEADS, length, length), bf16),
            pltpu.VMEM((length, width), f32),
            pltpu.VMEM((3, rows, width), bf16),
            pltpu.VMEM((4, 8, width), f32),
            pltpu.VMEM((rows, width), f32),
            pltpu.SemaphoreType.DMA((2,)),
            pltpu.SemaphoreType.DMA((micro_count,)),
            pltpu.SemaphoreType.DMA((2,)),
            pltpu.SemaphoreType.DMA((micro_count,)),
            pltpu.SemaphoreType.DMA,
        ],
        compiler_params=pltpu.CompilerParams(
            vmem_limit_bytes=63 << 20,
            **({"collective_id": 0, "has_side_effects": True} if stages > 1 else {}),
        ),
    )(token_ids, order, timesteps, table, gain, bias, w_qkv, w_out, w_in, w_down)


def body(token_ids, order, timesteps, table, norm_gain, norm_bias, w_qkv, w_out, w_in, w_down):
    stages = lax.axis_size("section")
    vocab = table.shape[0]
    bf16, f32 = jnp.bfloat16, jnp.float32
    gathered = (
        lax.all_gather(norm_gain[0].astype(bf16), "dp", axis=1, tiled=True).astype(f32),
        lax.all_gather(norm_bias[0].astype(bf16), "dp", axis=1, tiled=True).astype(f32),
        lax.all_gather(w_qkv[0].astype(bf16), "dp", axis=0, tiled=True),
        lax.all_gather(w_out[0].astype(bf16), "dp", axis=0, tiled=True),
        lax.all_gather(w_in[0].astype(bf16), "dp", axis=0, tiled=True),
        lax.all_gather(w_down[0].astype(bf16), "dp", axis=0, tiled=True),
    )
    sums = run_pipeline(stages, token_ids, order, timesteps[:, :, None], table, gathered)
    shared = [
        lax.psum_scatter(value.astype(bf16), "dp", scatter_dimension=axis, tiled=True)
        .astype(f32)[None]
        for value, axis in zip(sums[1:7], (1, 1, 0, 0, 0, 0))
    ]
    table_part = lax.psum_scatter(
        sums[0][:vocab].astype(bf16), "section", scatter_dimension=1, tiled=True
    ).astype(f32)
    return (lax.psum(table_part, "dp"), *shared)


def solution(mesh):
    in_specs = (
        P(None, "dp", None),
        P(None, "dp", None),
        P(None, "dp"),
        P(),
        P("section", None, "dp"),
        P("section", None, "dp"),
        P("section", "dp", None),
        P("section", "dp", None),
        P("section", "dp", None),
        P("section", "dp", None),
    )
    out_specs = (
        P(None, "section"),
        P("section", None, "dp"),
        P("section", None, "dp"),
        P("section", "dp", None),
        P("section", "dp", None),
        P("section", "dp", None),
        P("section", "dp", None),
    )
    return jax.shard_map(body, mesh=mesh, in_specs=in_specs, out_specs=out_specs, check_vma=False)
```

time: 1670 us -> 602 us (0.36)
  waiting for transfers between devices: 778 us -> 291 us
  matrix products: 349 us -> 0 us
  Pallas kernels: 0 us -> 209 us
  starting transfers between devices: 192 us -> 0.42 us
  other arithmetic: 150 us -> 28.3 us
  local copies, waits for them, and re-layouts: 120 us -> 6.42 us
    ppermute x30 -> x0, waiting for transfers between devices: 494 us -> none  [shifted_2(): return lax.ppermute(block, axis, route)]
    dot_general x200 -> x0, matrix products: 335 us -> none  [the longest x48 116 us: matmul_rows(): jnp.einsum('btd,de->bte', left, right, preferred_element_type=jnp.float32)]
    pallas_call x0 -> x1, Pallas kernels: none -> 209 us  [run_pipeline(): pl.pallas_call(functools.partial(pipeline_kernel, stages), out_shape=outs...]
    ppermute x30 -> x0, starting transfers between devices: 192 us -> none  [shifted_2(): return lax.ppermute(block, axis, route)]
    reduce_sum x80 -> x0, other arithmetic: 56 us -> none  [the longest x40 24.1 us: unit_rows(): variance = jnp.mean(centered * centered, axis=-1, keepdims=True)]
    cond x592 -> x0, local copies, waits for them, and re-layouts: 50.8 us -> none
    broadcast_in_dim x22 -> x1, local copies, waits for them, and re-layouts: 22.3 us -> 0.67 us  [body(): timesteps[:, :, None]]
    convert_element_type x24 -> x0, local copies, waits for them, and re-layouts: 18.7 us -> none  [the longest x8 14.4 us: layer_backward(): grad_mixed = matmul_back(grad_attended, w_out).astype(jnp.bfloat16).resha...]
  transfers between devices with their start and end apart: 40 -> 10, of which waited for: 39 -> 10; matrix products, arithmetic and copies ran while one was open for 2% -> 5% of each run, Pallas kernels for 0% -> 0%
where the time goes in v1:
time: 602 us; the launch traced here: 601 us
  waiting for transfers between devices  291 us (48%)
  Pallas kernels  209 us (35%)
  blocking collectives  51.8 us (9%)
  other arithmetic  28.3 us (5%)
  between operations  14.3 us (2%)
  local copies, waits for them, and re-layouts  6.42 us (1%)
    pallas_call x1, Pallas kernels, run_pipeline(): pl.pallas_call(functools.partial(pipeline_kernel, stages), out_shape=outs...  209 us
    reduce_scatter x4, waiting for transfers between devices, body(): lax.psum_scatter(value.astype(bf16), 'dp', scatter_dimension=axis, tiled=...  129 us
    unnamed x13, waiting for transfers between devices  58.9 us
    all_gather x1, waiting for transfers between devices, body(): lax.all_gather(w_in[0].astype(bf16), 'dp', axis=0, tiled=True)  47.1 us
    all_gather x1, waiting for transfers between devices, body(): lax.all_gather(w_down[0].astype(bf16), 'dp', axis=0, tiled=True)  46.9 us
    all_gather x1, blocking collectives, body(): lax.all_gather(w_out[0].astype(bf16), 'dp', axis=0, tiled=True)  19.7 us
    psum x1, blocking collectives, body(): return (lax.psum(table_part, 'dp'), *shared)  16.3 us
    convert_element_type x6, other arithmetic, body(): value.astype(bf16)  14.3 us
  transfers between devices with their start and end apart: 10, of which 10 were waited for; matrix products, arithmetic and copies ran while one was open for 5% of the time, Pallas kernels for 0%

profile of v1, /device:TPU:1, one launch (start us, length us, event | category | flops | bytes accessed | tf_op | source)
XLA Modules:
  0.0 600.8 jit_solution(15447532728703081270)
XLA Ops:
  7.2 2.1 convert_element_type.76
  9.4 0.0 all-gather.12.cloned.1.call-start
  9.4 0.9 convert_element_type.80
  10.3 0.0 all-gather.14.cloned.1.call-start
  10.4 0.9 convert_element_type.82
  11.3 0.0 reduce-scatter.26.cloned.1.call-start
  11.4 0.7 copy.18.stamp_ref
  12.1 9.9 %all-gather.1 = bf16[1,2,512]{2,1,0:T(2,128)(2,1)S(1)} all-gather(bf16[1,2,128]{2,1,0:T(2,128)(2,1)S(1)} %convert_element_type.73), channel_id=3, replica_groups=mesh['section'=8,'dp'=4] {'dp'}, dimensions={2}, use_global_device_ids=true | all-gather | bytes 2560 | tf_op jit(solution)/shard_map/all_gather | solution.py:426
  22.0 5.9 all-gather
  27.9 19.7 %all-gather.3 = bf16[1,512,512]{2,1,0:T(8,128)(2,1)} all-gather(bf16[1,128,512]{2,1,0:T(8,128)(2,1)S(1)} %convert_element_type.78), channel_id=5, replica_groups=mesh['section'=8,'dp'=4] {'dp'}, dimensions={1}, use_global_device_ids=true | all-gather | bytes 655360 | tf_op jit(solution)/shard_map/all_gather | solution.py:428
  47.6 0.6 bitcast_convert_fusion.5.gain_ref
  48.2 0.6 bitcast_convert_fusion.4.bias_ref
  48.8 8.9 %all-gather.10.cloned.1.call-done = bf16[1,512,1536]{2,1,0:T(8,128)(2,1)} async-done(((bf16[1,128,1536]{2,1,0:T(8,128)(2,1)}), bf16[1,512,1536]{2,1,0:T(8,128)(2,1)}) %all-gather.10.cloned.1.call-update) | async-done | bytes 1572880 | tf_op jit(solution)/shard_map/all_gather | solution.py:427
  57.7 47.1 %all-gather.12.cloned.1.call-done = bf16[1,512,2048]{2,1,0:T(8,128)(2,1)} async-done(((bf16[1,128,2048]{2,1,0:T(8,128)(2,1)}), bf16[1,512,2048]{2,1,0:T(8,128)(2,1)}) %all-gather.12.cloned.1.call-update) | async-done | bytes 2097168 | tf_op jit(solution)/shard_map/all_gather | solution.py:429
  104.8 46.9 %all-gather.14.cloned.1.call-done = bf16[1,2048,512]{2,1,0:T(8,128)(2,1)} async-done(((bf16[1,512,512]{2,1,0:T(8,128)(2,1)}), bf16[1,2048,512]{2,1,0:T(8,128)(2,1)}) %all-gather.14.cloned.1.call-update) | async-done | bytes 2097168 | tf_op jit(solution)/shard_map/all_gather | solution.py:430
  151.6 209.0 %shard_map.153 = (f32[32,512]{1,0:T(8,128)}, f32[2,512]{1,0:T(2,128)}, f32[2,512]{1,0:T(2,128)}, f32[512,1536]{1,0:T(8,128)}, f32[512,512]{1,0:T(8,128)}, /*inde...) custom-call(s32[8,1,256]{2,1,0:T(1,128)} %token_ref.1, s32[8,1,256]{2,1,0:T(1,128)} %order_ref.1, ...), custom_call_target="tpu_custom_call" | custom-call | tf_op jit(solution)/shard_map/pallas_call | solution.py:386
  360.7 0.7 convert_element_type.86
  361.3 0.8 copy.23
  362.2 0.0 reduce-scatter.24.cloned.1.call-start
  362.2 0.7 convert_element_type.85
  362.9 0.8 copy.21
  363.8 0.0 reduce-scatter.22.cloned.1.call-start
  363.8 0.8 slice.7
  364.6 0.8 copy.19
  365.5 0.0 reduce-scatter.16.cloned.1.call-start
  365.5 2.1 convert_element_type.88
  367.6 0.0 reduce-scatter.14.cloned.1.call-start
  367.7 3.2 convert_element_type.87
  370.9 0.0 reduce-scatter.18.cloned.1.call-start
  371.0 3.9 convert_element_type.89
  374.9 3.8 convert_element_type.90
  378.7 4.6 reduce-scatter.26.cloned.1.call-done
  383.3 0.8 copy.24
  384.1 19.3 %reduce-scatter.24.cloned.1.call-done = bf16[128,2]{1,0:T(8,128)(2,1)} async-done(((bf16[512,2]{1,0:T(8,128)(2,1)}), bf16[128,2]{1,0:T(8,128)(2,1)}) %reduce-scatter.24.cloned.1.call-update) | async-done | bytes 528
  403.4 0.8 copy.22
  404.3 0.6 bitcast_convert_fusion.6
  404.8 0.6 bitcast_convert_fusion.7
  405.4 34.8 %reduce-scatter.22.cloned.1.call-done = bf16[64,28]{1,0:T(8,128)(2,1)} async-done(((bf16[512,28]{1,0:T(8,128)(2,1)}), bf16[64,28]{1,0:T(8,128)(2,1)}) %reduce-scatter.22.cloned.1.call-update) | async-done | bytes 3600
  440.3 0.8 copy.20
  441.1 16.3 %psum.7 = f32[28,64]{1,0:T(8,128)} all-reduce(bf16[28,64]{1,0:T(8,128)(2,1)S(1)} %copy.20), channel_id=1, replica_groups=mesh['section'=8,'dp'=4] {'dp'}, use_global_device_ids=true, to_apply=%region_1.0 | all-reduce | flops 1792 | bytes 10752 | tf_op jit(solution)/shard_map/psum | solution.py:441
  457.4 6.0 %reduce-scatter.16.cloned.1.call-done = bf16[128,512]{1,0:T(8,128)(2,1)} async-done(((bf16[512,512]{1,0:T(8,128)(2,1)}), bf16[128,512]{1,0:T(8,128)(2,1)}) %reduce-scatter.16.cloned.1.call-update) | async-done | bytes 131088 | tf_op jit(solution)/shard_map/reduce_scatter | solution.py:434
  463.4 1.6 bitcast_convert_fusion.3
  465.0 36.1 %reduce-scatter.14.cloned.1.call-done = bf16[128,1536]{1,0:T(8,128)(2,1)} async-done(((bf16[512,1536]{1,0:T(8,128)(2,1)}), bf16[128,1536]{1,0:T(8,128)(2,1)}) %reduce-scatter.14.cloned.1.call-update) | async-done | bytes 393232 | tf_op jit(solution)/shard_map/reduce_scatter | solution.py:434
  501.1 2.0 bitcast_convert_fusion.2
  503.1 43.3 %reduce-scatter.18.cloned.1.call-done = bf16[128,2048]{1,0:T(8,128)(2,1)} async-done(((bf16[512,2048]{1,0:T(8,128)(2,1)}), bf16[128,2048]{1,0:T(8,128)(2,1)}) %reduce-scatter.18.cloned.1.call-update) | async-done | bytes 524304 | tf_op jit(solution)/shard_map/reduce_scatter | solution.py:434
  546.4 2.1 bitcast_convert_fusion.1
  548.5 43.3 %reduce-scatter.20.cloned.1.call-done = bf16[512,512]{1,0:T(8,128)(2,1)} async-done(((bf16[2048,512]{1,0:T(8,128)(2,1)}), bf16[512,512]{1,0:T(8,128)(2,1)}) %reduce-scatter.20.cloned.1.call-update) | async-done | bytes 524304 | tf_op jit(solution)/shard_map/reduce_scatter | solution.py:434
  591.8 2.1 bitcast_convert_fusion
  (27 shorter events, 0.3 us)
Async XLA Ops:
  7.2 2.2 copy-start
  7.2 3.2 copy-start.1
  7.2 50.5 %all-gather.10.cloned.1.call-start = ((), (), s32[]{:S(2)}) async-start(), calls=%async_computation.11 | async-start | bytes 1966080 | tf_op jit(solution)/shard_map/all_gather | solution.py:427
  9.3 2.0 copy-start.4
  9.3 2.0 copy-start.5
  9.3 2.0 copy-start.3
  9.4 2.7 copy-start.2
  9.4 95.4 %all-gather.12.cloned.1.call-start = ((), (), s32[]{:S(2)}) async-start(), calls=%async_computation.12 | async-start | bytes 2621440 | tf_op jit(solution)/shard_map/all_gather | solution.py:429
  10.3 141.3 %all-gather.14.cloned.1.call-start = ((), (), s32[]{:S(2)}) async-start(), calls=%async_computation.13 | async-start | bytes 2621440 | tf_op jit(solution)/shard_map/all_gather | solution.py:430
  11.3 372.1 %reduce-scatter.26.cloned.1.call-start = ((), (), s32[]{:S(2)}) async-start(), calls=%async_computation.16 | async-start | bytes 163840
  362.2 41.3 %reduce-scatter.24.cloned.1.call-start = ((), (), s32[]{:S(2)}) async-start(), calls=%async_computation.15 | async-start | bytes 163840
  363.8 76.5 %reduce-scatter.22.cloned.1.call-start = ((), (), s32[]{:S(2)}) async-start(), calls=%async_computation.14 | async-start | bytes 147456
  365.5 97.9 %reduce-scatter.16.cloned.1.call-start = ((), (), s32[]{:S(2)}) async-start(), calls=%async_computation.8 | async-start | bytes 655360 | tf_op jit(solution)/shard_map/reduce_scatter | solution.py:434
  367.6 133.5 %reduce-scatter.14.cloned.1.call-start = ((), (), s32[]{:S(2)}) async-start(), calls=%async_computation.7 | async-start | bytes 1966080 | tf_op jit(solution)/shard_map/reduce_scatter | solution.py:434
  370.9 175.5 %reduce-scatter.18.cloned.1.call-start = ((), (), s32[]{:S(2)}) async-start(), calls=%async_computation.9 | async-start | bytes 2621440 | tf_op jit(solution)/shard_map/reduce_scatter | solution.py:434
  374.9 216.9 %reduce-scatter.20.cloned.1.call-start = ((), (), s32[]{:S(2)}) async-start(), calls=%async_computation.10 | async-start | bytes 2621440 | tf_op jit(solution)/shard_map/reduce_scatter | solution.py:434
Sparse Core Ops, SparseCore 0:
  10.2 47.4 all-gather.9
  59.8 44.9 all-gather.11
  106.9 44.6 all-gather.13
  362.3 20.9 reduce-scatter.25
  386.1 17.3 reduce-scatter.23
  406.9 33.3 reduce-scatter.21
  443.2 20.1 reduce-scatter.15
  465.8 35.2 reduce-scatter.13
  503.5 42.8 reduce-scatter.17
  548.6 43.1 reduce-scatter.19

commit v2 on v1

--- a/solution.py
+++ b/solution.py
@@ -12,6 +12,7 @@
 EPSILON = 1e-05
 EMBED_GAIN = 16.0
 FF_CHUNK = 512
+NORM_ROWS = 8
 MESH = pl.DeviceIdType.MESH
 
 
@@ -40,26 +41,61 @@
     return jnp.sum(values.reshape(rows // 8, 8, columns), axis=0)
 
 
+def chip_of(place, row, per_plane):
+    return row * per_plane + lax.rem(place - lax.rem(row, per_plane) + per_plane, per_plane)
+
+
+def start_copy(src, dst, send_sem, recv_sem, device, here):
+    section, plane = device
+    same = jnp.logical_and(section == here[0], plane == here[1])
+
+    @pl.when(same)
+    def _():
+        pltpu.make_async_copy(src, dst, recv_sem).start()
+
+    @pl.when(jnp.logical_not(same))
+    def _():
+        remote_copy(src, dst, send_sem, recv_sem, device).start()
+
+
+def wait_sent(src, dst, send_sem, recv_sem, device, here):
+    section, plane = device
+    same = jnp.logical_and(section == here[0], plane == here[1])
+
+    @pl.when(jnp.logical_not(same))
+    def _():
+        remote_copy(src, dst, send_sem, recv_sem, device).wait_send()
+
+
+def remote_copy(src, dst, send_sem, recv_sem, device):
+    return pltpu.make_async_remote_copy(
+        src_ref=src,
+        dst_ref=dst,
+        send_sem=send_sem,
+        recv_sem=recv_sem,
+        device_id={"section": device[0], "dp": device[1]},
+        device_id_type=MESH,
+    )
+
+
 def pipeline_kernel(
     stages,
+    planes,
+    token_in_ref,
+    table_ref,
+    norm_shard,
+    qkv_shard,
+    out_shard,
+    in_shard,
+    down_shard,
+    d_table_ref,
+    norm_total,
+    qkv_total,
+    out_total,
+    in_total,
+    down_total,
+    stash_ref,
     token_ref,
-    order_ref,
-    stamp_ref,
-    table_ref,
-    gain_ref,
-    bias_ref,
-    w_qkv_ref,
-    w_out_ref,
-    w_in_ref,
-    w_down_ref,
-    d_table_ref,
-    d_gain_ref,
-    d_bias_ref,
-    d_qkv_ref,
-    d_out_ref,
-    d_in_ref,
-    d_down_ref,
-    stash_ref,
     h_in,
     g_in,
     h_send,
@@ -75,11 +111,39 @@
     table_parts,
     norm_sums,
     table_sum,
+    norm_slots,
+    norm_full,
+    w_qkv_ref,
+    w_out_ref,
+    w_in_ref,
+    w_down_ref,
+    gain_ref,
+    bias_ref,
+    d_norm_ref,
+    d_qkv_ref,
+    d_out_ref,
+    d_in_ref,
+    d_down_ref,
     h_send_sem,
     h_recv_sem,
     g_send_sem,
     g_recv_sem,
     stash_sem,
+    token_send_sem,
+    token_recv_sem,
+    load_sem,
+    spread_send,
+    spread_recv,
+    plane_send,
+    plane_recv,
+    peer_send,
+    peer_recv,
+    core_send,
+    core_recv,
+    core_free,
+    peer_free,
+    total_send,
+    total_recv,
 ):
     micro_count, _, length = token_ref.shape
     vocab, width = table_ref.shape
@@ -87,18 +151,268 @@
     head_size = width // HEADS
     score_scale = 1.0 / math.sqrt(head_size)
     pair_width = 2 * head_size
-    stage = lax.axis_index("section")
+    bf16, f32 = jnp.bfloat16, jnp.float32
+
+    per_plane, rows = stages // planes, planes // 2
+    section, plane = lax.axis_index("section"), lax.axis_index("dp")
+    here = (section, plane)
+    chip, core = lax.div(section, 2), lax.rem(section, 2)
+    row = lax.div(chip, per_plane)
+    place = lax.rem(lax.rem(chip, per_plane) + row, per_plane)
+    odd = lax.rem(plane, 2)
+    turn = jnp.where(odd == 0, place, per_plane - 1 - place)
+    stage = plane * per_plane + turn
     last = stages - 1
-    bf16, f32 = jnp.bfloat16, jnp.float32
-
-    if stages > 1:
-        ahead, behind = lax.rem(stage + 1, stages), lax.rem(stage + stages - 1, stages)
-        barrier = pltpu.get_barrier_semaphore()
-        for neighbour in (ahead, behind):
+    lane_row = lax.rem(row - lax.rem(place, rows) * core + rows, rows)
+    lane_index = 2 * lane_row + core
+
+    def next_device():
+        step = jnp.where(odd == 0, 1, -1)
+        near_place = place + step
+        near_row = lax.rem(row + core * step + rows, rows)
+        near = 2 * chip_of(near_place + per_plane, near_row, per_plane) + core
+        stays = turn < per_plane - 1
+        return jnp.where(stays, near, section), jnp.where(stays, plane, plane + 1)
+
+    def previous_device():
+        step = jnp.where(odd == 0, -1, 1)
+        near_place = place + step
+        near_row = lax.rem(row + core * step + rows, rows)
+        near = 2 * chip_of(near_place + per_plane, near_row, per_plane) + core
+        stays = turn > 0
+        return jnp.where(stays, near, section), jnp.where(stays, plane, plane - 1)
+
+    ahead, behind = next_device(), previous_device()
+    partner = (section + 1 - 2 * core, plane)
+
+    def layer_device(layer, at_row, at_core):
+        at_plane, at_turn = lax.div(layer, per_plane), lax.rem(layer, per_plane)
+        at_place = jnp.where(lax.rem(at_plane, 2) == 0, at_turn, per_plane - 1 - at_turn)
+        return 2 * chip_of(at_place, at_row, per_plane) + at_core, at_plane
+
+    def layer_here(at_plane):
+        at_turn = jnp.where(at_plane % 2 == 0, place, per_plane - 1 - place)
+        return at_plane * per_plane + at_turn
+
+    def peer(at_row):
+        return layer_device(stage, at_row, core)
+
+    home_plane = lax.div(section, per_plane)
+    carries = lax.rem(plane, 2) == core
+
+    barrier = pltpu.get_barrier_semaphore()
+    greetings = []
+
+    def greet(device, wanted=True):
+        same = jnp.logical_and(device[0] == section, device[1] == plane)
+        wanted = jnp.logical_and(wanted, jnp.logical_not(same))
+        greetings.append(jnp.where(wanted, 1, 0))
+
+        @pl.when(wanted)
+        def _():
             pl.semaphore_signal(
-                barrier, inc=1, device_id={"section": neighbour}, device_id_type=MESH
+                barrier,
+                inc=1,
+                device_id={"section": device[0], "dp": device[1]},
+                device_id_type=MESH,
             )
-        pl.semaphore_wait(barrier, 2)
+
+    for other in range(planes):
+        greet((section, other))
+        greet((layer_here(other), plane), carries)
+    for at_row in range(rows):
+        owner = layer_device(section, at_row, lax.rem(plane, 2))
+        greet((owner[0], plane))
+        greet(owner)
+        greet((stage, 2 * at_row + core))
+        greet(peer(at_row))
+    greet(partner)
+    greet(ahead, stage < last)
+    greet(behind, stage > 0)
+    pl.semaphore_wait(barrier, sum(greetings))
+
+    matrices = (
+        (w_qkv_ref, d_qkv_ref, qkv_shard, qkv_total, packed),
+        (w_out_ref, d_out_ref, out_shard, out_total, mixed),
+        (w_in_ref, d_in_ref, in_shard, in_total, active),
+        (w_down_ref, d_down_ref, down_shard, down_total, middle),
+        (norm_full, d_norm_ref, norm_shard, norm_total, norm_slots),
+    )
+    count = len(matrices)
+    norms = count - 1
+    heights = [matrix[0].shape[0] // (planes * rows) for matrix in matrices]
+
+    def slot(matrix, index):
+        buffer, height = matrices[matrix][4], heights[matrix]
+        per_block = buffer.shape[1] // height
+        block, inside = index // per_block, index % per_block
+        if not isinstance(inside, int):
+            inside = pl.multiple_of(inside * height, height)
+        else:
+            inside = inside * height
+        return buffer.at[block, pl.ds(inside, height)]
+
+    def piece(matrix, quarter, at_row):
+        height = heights[matrix]
+        return pl.ds(pl.multiple_of((quarter * rows + at_row) * height, height), height)
+
+    gives_tokens = jnp.logical_and(place == 0, lane_index == plane)
+    takes_tokens = jnp.logical_or(stage == 0, stage == last)
+
+    def token_copy(index, target):
+        return (
+            token_in_ref,
+            token_ref,
+            token_send_sem.at[index],
+            token_recv_sem,
+            (section, target),
+        )
+
+    @pl.when(gives_tokens)
+    def _():
+        for index, target in enumerate((0, planes - 1)):
+            start_copy(*token_copy(index, target), here)
+
+    loads = []
+    for matrix in range(norms):
+        shard, landing = matrices[matrix][2], matrices[matrix][1]
+        loads.append(
+            pltpu.make_async_copy(
+                shard.at[0], landing.at[pl.ds(0, shard.shape[1])], load_sem.at[matrix]
+            )
+        )
+        loads[-1].start()
+
+    def spread_args(matrix, at_row):
+        target, _ = layer_device(section, at_row, lax.rem(plane, 2))
+        if matrix == norms:
+            source = norm_shard.at[pl.ds(at_row * NORM_ROWS, NORM_ROWS)]
+        else:
+            source = slot(matrix, planes + at_row)
+        return (
+            source,
+            slot(matrix, home_plane),
+            spread_send.at[matrix, at_row],
+            spread_recv.at[matrix, home_plane],
+            (target, plane),
+        )
+
+    def plane_args(matrix, to_plane, from_plane):
+        return (
+            slot(matrix, to_plane),
+            matrices[matrix][0].at[piece(matrix, from_plane, row)],
+            plane_send.at[matrix, to_plane],
+            plane_recv.at[matrix, lax.div(from_plane, 2)],
+            (section, to_plane),
+        )
+
+    def peer_args(matrix, quarter_pair, from_row, to_row):
+        part = matrices[matrix][0].at[piece(matrix, 2 * quarter_pair + core, from_row)]
+        return (
+            part,
+            part,
+            peer_send.at[matrix, quarter_pair, to_row],
+            peer_recv.at[matrix, quarter_pair, from_row],
+            peer(to_row),
+        )
+
+    def core_args(matrix, quarter_pair, at_row, from_core):
+        part = matrices[matrix][0].at[piece(matrix, 2 * quarter_pair + from_core, at_row)]
+        return (
+            part,
+            part,
+            core_send.at[matrix, quarter_pair, at_row],
+            core_recv.at[matrix, quarter_pair, at_row],
+            partner,
+        )
+
+    def spread(matrix):
+        if matrix != norms:
+            loads[matrix].wait()
+            for at_row in range(rows):
+                height = heights[matrix]
+                source = matrices[matrix][1][at_row * height : (at_row + 1) * height, :]
+                slot(matrix, planes + at_row)[...] = source.astype(bf16)
+        for at_row in range(rows):
+            start_copy(*spread_args(matrix, at_row), here)
+
+    def along_planes(matrix):
+        @pl.when(carries)
+        def _():
+            for to_plane in range(planes):
+                remote_copy(
+                    slot(matrix, to_plane),
+                    slot(matrix, to_plane),
+                    spread_send.at[matrix, 0],
+                    spread_recv.at[matrix, to_plane],
+                    partner,
+                ).wait_recv()
+                start_copy(*plane_args(matrix, to_plane, plane), here)
+
+    def between_peers(matrix):
+        for pair in range(rows):
+            remote_copy(*plane_args(matrix, 0, 2 * pair + core)).wait_recv()
+            for to_row in range(rows):
+                @pl.when(to_row != row)
+                def _():
+                    remote_copy(*peer_args(matrix, pair, row, to_row)).start()
+
+            remote_copy(*core_args(matrix, pair, row, core)).start()
+
+    def between_cores(matrix):
+        for pair in range(rows):
+            for from_row in range(rows):
+                @pl.when(from_row != row)
+                def _():
+                    remote_copy(*peer_args(matrix, pair, from_row, from_row)).wait_recv()
+                    remote_copy(*core_args(matrix, pair, from_row, core)).start()
+
+    def gathered(matrix):
+        for pair in range(rows):
+            for at_row in range(rows):
+                remote_copy(*core_args(matrix, pair, at_row, 1 - core)).wait_recv()
+
+    def gather_sent(matrix):
+        for at_row in range(rows):
+            wait_sent(*spread_args(matrix, at_row), here)
+
+        @pl.when(carries)
+        def _():
+            for to_plane in range(planes):
+                wait_sent(*plane_args(matrix, to_plane, plane), here)
+
+        for pair in range(rows):
+            for at_row in range(rows):
+                @pl.when(at_row != row)
+                def _():
+                    remote_copy(*peer_args(matrix, pair, row, at_row)).wait_send()
+
+                remote_copy(*core_args(matrix, pair, at_row, core)).wait_send()
+
+    steps_of_gather = (spread, along_planes, between_peers, between_cores, gathered)
+    order = (norms, 0, 1, 2, 3)
+    for turn_at in range(count + len(steps_of_gather) - 1):
+        for depth, action in enumerate(steps_of_gather):
+            if 0 <= turn_at - depth < count:
+                action(order[turn_at - depth])
+    for matrix in range(count):
+        gather_sent(matrix)
+
+    @pl.when(takes_tokens)
+    def _():
+        remote_copy(*token_copy(0, 0)).wait_recv()
+
+    @pl.when(gives_tokens)
+    def _():
+        for index, target in enumerate((0, planes - 1)):
+            wait_sent(*token_copy(index, target), here)
+
+    for kind, ref in enumerate((gain_ref, bias_ref)):
+        total = jnp.zeros((NORM_ROWS, width), f32)
+        for quarter in range(planes):
+            start = (quarter * rows + kind) * NORM_ROWS
+            total = total + norm_full[start : start + NORM_ROWS, :]
+        ref[...] = total.astype(bf16).astype(f32)
 
     table_rows = table_parts.shape[1]
     work[:table_rows, :] = jnp.zeros((table_rows, width), f32)
@@ -120,8 +434,9 @@
     lower = lane < head_size
 
     def shown_rows(micro):
-        visible = order_ref[micro] < stamp_ref[micro]
-        shown = jnp.where(visible, token_ref[micro], vocab - 1)
+        rows_of = token_ref[micro]
+        visible = rows_of[1:2] < rows_of[2:3]
+        shown = jnp.where(visible, rows_of[0:1], vocab - 1)
         return (letters == shown).astype(bf16)
 
     def halves(pair):
@@ -148,7 +463,7 @@
             dst_ref=h_in.at[micro],
             send_sem=h_send_sem.at[slot],
             recv_sem=h_recv_sem.at[micro],
-            device_id={"section": target},
+            device_id={"section": target[0], "dp": target[1]},
             device_id_type=MESH,
         )
 
@@ -159,7 +474,7 @@
             dst_ref=g_in.at[micro],
             send_sem=g_send_sem.at[slot],
             recv_sem=g_recv_sem.at[micro],
-            device_id={"section": target},
+            device_id={"section": target[0], "dp": target[1]},
             device_id_type=MESH,
         )
 
@@ -194,8 +509,8 @@
         save.start()
         between = hidden + dot(mixed[micro], w_out_ref[...], 1, 0)
         high = between.astype(bf16)
-        middle[micro, 0] = high
-        middle[micro, 1] = (between - high.astype(f32)).astype(bf16)
+        middle[2 * micro + 0] = high
+        middle[2 * micro + 1] = (between - high.astype(f32)).astype(bf16)
         work[...] = between
         unit, _ = unit_rows(between)
         normed_two = (unit * gain_ref[1:2, :] + bias_ref[1:2, :]).astype(bf16)
@@ -230,11 +545,10 @@
         largest = jnp.max(logits, axis=0, keepdims=True)
         powers = jnp.exp(logits - largest)
         total = jnp.sum(powers, axis=0, keepdims=True)
-        stamp = stamp_ref[micro]
-        weight = jnp.where(
-            order_ref[micro] < stamp, 0.0, 1.0 / (length - stamp).astype(f32)
-        )
-        target = (letters == token_ref[micro]).astype(f32)
+        rows_of = token_ref[micro]
+        stamp = rows_of[2:3]
+        weight = jnp.where(rows_of[1:2] < stamp, 0.0, 1.0 / (length - stamp).astype(f32))
+        target = (letters == rows_of[0:1]).astype(f32)
         g_logits = (weight * (powers / total - target)).astype(bf16)
         table_sum[...] += dot(g_logits, rounded, 1, 0)
         g_unit = dot(g_logits, table_parts[0], 0, 0)
@@ -258,13 +572,13 @@
                 g_active * slope[micro, :, at : at + FF_CHUNK].astype(f32)
             ).astype(bf16)
         g_normed = dot(slope[micro], w_in_ref[...], 1, 1)
-        unit, scale = unit_rows(middle[micro, 0].astype(f32) + middle[micro, 1].astype(f32))
-        middle[micro, 0] = (unit * gain_ref[1:2, :] + bias_ref[1:2, :]).astype(bf16)
+        unit, scale = unit_rows(middle[2 * micro + 0].astype(f32) + middle[2 * micro + 1].astype(f32))
+        middle[2 * micro + 0] = (unit * gain_ref[1:2, :] + bias_ref[1:2, :]).astype(bf16)
         norm_sums[1] += fold_rows(g_normed * unit)
         norm_sums[3] += fold_rows(g_normed)
         g_middle = g_out.astype(f32) + unit_back(g_normed * gain_ref[1:2, :], unit, scale)
         g_attended = g_middle.astype(bf16)
-        middle[micro, 1] = g_attended
+        middle[2 * micro + 1] = g_attended
         g_mixed = dot(g_attended, w_out_ref[...], 1, 1).astype(bf16)
         load_hidden(micro)
         load.wait()
@@ -321,8 +635,8 @@
 
     def weights(micro):
         d_down_ref[...] += dot(active[micro], g_in[micro], 0, 0)
-        d_in_ref[...] += dot(middle[micro, 0], slope[micro], 0, 0)
-        d_out_ref[...] += dot(mixed[micro], middle[micro, 1], 0, 0)
+        d_in_ref[...] += dot(middle[2 * micro + 0], slope[micro], 0, 0)
+        d_out_ref[...] += dot(mixed[micro], middle[2 * micro + 1], 0, 0)
         d_qkv_ref[...] += dot(h_in[micro], packed[micro], 0, 0)
 
     steps = max(2 * last + micro_count, last + 2 * micro_count)
@@ -359,86 +673,228 @@
                 gradient_copy(micro, behind).wait_send()
 
     d_table_ref[...] = table_sum[...]
-    for member in range(2):
-        d_gain_ref[member : member + 1, :] = jnp.sum(norm_sums[member], axis=0, keepdims=True)
-        d_bias_ref[member : member + 1, :] = jnp.sum(norm_sums[2 + member], axis=0, keepdims=True)
-
-
-def run_pipeline(stages, token_ids, order, timesteps, table, gathered):
-    gain, bias, w_qkv, w_out, w_in, w_down = gathered
-    micro_count, _, length = token_ids.shape
+    for kind in range(2):
+        totals = [
+            jnp.sum(norm_sums[2 * kind + member], axis=0, keepdims=True) for member in range(2)
+        ]
+        block = jnp.concatenate(totals + [jnp.zeros((NORM_ROWS - 2, width), f32)], axis=0)
+        for quarter in range(planes):
+            start = (quarter * rows + kind) * NORM_ROWS
+            d_norm_ref[start : start + NORM_ROWS, :] = block
+
+    pl.semaphore_signal(
+        core_free, inc=1, device_id={"section": partner[0], "dp": partner[1]}, device_id_type=MESH
+    )
+    for at_row in range(rows):
+        @pl.when(at_row != row)
+        def _():
+            far = peer(at_row)
+            pl.semaphore_signal(
+                peer_free, inc=1, device_id={"section": far[0], "dp": far[1]}, device_id_type=MESH
+            )
+
+    def core_sum_args(matrix, pair, at_row):
+        index = pair * rows + at_row
+        return (
+            slot(matrix, index),
+            slot(matrix, rows * rows + index),
+            core_send.at[matrix, pair, at_row],
+            core_recv.at[matrix, pair, at_row],
+            partner,
+        )
+
+    def peer_sum_args(matrix, pair, from_row, to_row):
+        return (
+            slot(matrix, 2 * rows * rows + pair * rows + to_row),
+            slot(matrix, 3 * rows * rows + pair * rows + from_row),
+            peer_send.at[matrix, pair, to_row],
+            peer_recv.at[matrix, pair, from_row],
+            peer(to_row),
+        )
+
+    def total_args(matrix, pair):
+        height = heights[matrix]
+        return (
+            slot(matrix, 2 * rows * rows + pair * rows + row),
+            matrices[matrix][3].at[pl.ds(pl.multiple_of(row * height, height), height)],
+            total_send.at[matrix, pair],
+            total_recv.at[matrix, row],
+            (stage, 2 * pair + core),
+        )
+
+    def give_core(matrix):
+        for pair in range(rows):
+            for at_row in range(rows):
+                args = core_sum_args(matrix, pair, at_row)
+                part = matrices[matrix][1][piece(matrix, 2 * pair + 1 - core, at_row), :]
+                args[0][...] = part.astype(args[0].dtype)
+                remote_copy(*args).start()
+
+    def give_peers(matrix):
+        for pair in range(rows):
+            for at_row in range(rows):
+                remote_copy(*core_sum_args(matrix, pair, at_row)).wait_recv()
+                landed = slot(matrix, rows * rows + pair * rows + at_row)
+                part = matrices[matrix][1].at[piece(matrix, 2 * pair + core, at_row)]
+                total = part[...] + landed[...].astype(f32)
+
+                @pl.when(at_row != row)
+                def _():
+                    args = peer_sum_args(matrix, pair, row, at_row)
+                    args[0][...] = total.astype(args[0].dtype)
+                    remote_copy(*args).start()
+
+                @pl.when(at_row == row)
+                def _():
+                    part[...] = total
+
+    def give_totals(matrix):
+        for pair in range(rows):
+            part = matrices[matrix][1].at[piece(matrix, 2 * pair + core, row)]
+            for from_row in range(rows):
+                @pl.when(from_row != row)
+                def _():
+                    remote_copy(*peer_sum_args(matrix, pair, from_row, from_row)).wait_recv()
+                    landed = slot(matrix, 3 * rows * rows + pair * rows + from_row)
+                    part[...] += landed[...].astype(f32)
+
+            args = total_args(matrix, pair)
+            args[0][...] = part[...].astype(args[0].dtype)
+            start_copy(*args, here)
+
+    def finish(matrix):
+        height = heights[matrix]
+        for from_row in range(rows):
+            part = matrices[matrix][3].at[pl.ds(from_row * height, height)]
+            remote_copy(
+                part, part, total_send.at[matrix, 0], total_recv.at[matrix, from_row], partner
+            ).wait_recv()
+        for pair in range(rows):
+            for at_row in range(rows):
+                remote_copy(*core_sum_args(matrix, pair, at_row)).wait_send()
+
+                @pl.when(at_row != row)
+                def _():
+                    remote_copy(*peer_sum_args(matrix, pair, row, at_row)).wait_send()
+
+            wait_sent(*total_args(matrix, pair), here)
+
+    order = (norms, 3, 2, 0, 1)
+    pl.semaphore_wait(core_free, 1)
+    for matrix in order:
+        give_core(matrix)
+    pl.semaphore_wait(peer_free, rows - 1)
+    for position in range(count + 1):
+        if position < count:
+            give_peers(order[position])
+        if position > 0:
+            give_totals(order[position - 1])
+    for matrix in order:
+        finish(matrix)
+
+
+def run_pipeline(stages, planes, tokens, table, norm_shard, w_qkv, w_out, w_in, w_down):
+    micro_count, _, length = tokens.shape
     width = table.shape[1]
-    hidden_units = w_in.shape[1]
-    rows = -(-table.shape[0] // 32) * 32
+    hidden_units = w_in.shape[2]
+    rows = planes // 2
+    table_rows = -(-table.shape[0] // 32) * 32
     bf16, f32 = jnp.bfloat16, jnp.float32
     vmem = pl.BlockSpec(memory_space=pltpu.VMEM)
+    anywhere = pl.BlockSpec(memory_space=pl.ANY)
+    shards = (w_qkv, w_out, w_in, w_down)
+    full = [(shard.shape[1] * planes, shard.shape[2]) for shard in shards]
+    norm_full = (planes * norm_shard.shape[0], width)
     outs = (
-        jax.ShapeDtypeStruct((rows, width), f32),
-        jax.ShapeDtypeStruct((2, width), f32),
-        jax.ShapeDtypeStruct((2, width), f32),
-        jax.ShapeDtypeStruct(w_qkv.shape, f32),
-        jax.ShapeDtypeStruct(w_out.shape, f32),
-        jax.ShapeDtypeStruct(w_in.shape, f32),
-        jax.ShapeDtypeStruct(w_down.shape, f32),
+        jax.ShapeDtypeStruct((table_rows, width), f32),
+        jax.ShapeDtypeStruct(norm_shard.shape, f32),
+        *(jax.ShapeDtypeStruct(shard.shape[1:], bf16) for shard in shards),
         jax.ShapeDtypeStruct((micro_count, HEADS, length, length), bf16),
     )
     rows_shape = (micro_count, length, width)
+    pieces = (5, rows, rows)
     return pl.pallas_call(
-        functools.partial(pipeline_kernel, stages),
+        functools.partial(pipeline_kernel, stages, planes),
         out_shape=outs,
-        in_specs=[vmem] * 10,
-        out_specs=[vmem] * 7 + [pl.BlockSpec(memory_space=pl.ANY)],
+        in_specs=[vmem] * 3 + [anywhere] * 4,
+        out_specs=[vmem] * 6 + [anywhere],
         scratch_shapes=[
+            pltpu.VMEM(tokens.shape, jnp.int32),
             pltpu.VMEM(rows_shape, bf16),
             pltpu.VMEM(rows_shape, bf16),
             pltpu.VMEM((2, length, width), bf16),
             pltpu.VMEM((2, length, width), bf16),
             pltpu.VMEM((micro_count, length, 3 * width), bf16),
             pltpu.VMEM(rows_shape, bf16),
-            pltpu.VMEM((micro_count, 2, length, width), bf16),
+            pltpu.VMEM((2 * micro_count, length, width), bf16),
             pltpu.VMEM((micro_count, length, hidden_units), bf16),
             pltpu.VMEM((micro_count, length, hidden_units), bf16),
             pltpu.VMEM((HEADS, length, length), bf16),
             pltpu.VMEM((HEADS, length, length), bf16),
             pltpu.VMEM((length, width), f32),
-            pltpu.VMEM((3, rows, width), bf16),
+            pltpu.VMEM((3, table_rows, width), bf16),
             pltpu.VMEM((4, 8, width), f32),
-            pltpu.VMEM((rows, width), f32),
+            pltpu.VMEM((table_rows, width), f32),
+            pltpu.VMEM((4 * rows * rows, NORM_ROWS, width), f32),
+            pltpu.VMEM(norm_full, f32),
+            *(pltpu.VMEM(shape, bf16) for shape in full),
+            pltpu.VMEM((NORM_ROWS, width), f32),
+            pltpu.VMEM((NORM_ROWS, width), f32),
+            pltpu.VMEM(norm_full, f32),
+            *(pltpu.VMEM(shape, f32) for shape in full),
             pltpu.SemaphoreType.DMA((2,)),
             pltpu.SemaphoreType.DMA((micro_count,)),
             pltpu.SemaphoreType.DMA((2,)),
             pltpu.SemaphoreType.DMA((micro_count,)),
             pltpu.SemaphoreType.DMA,
+            pltpu.SemaphoreType.DMA((2,)),
+            pltpu.SemaphoreType.DMA,
+            pltpu.SemaphoreType.DMA((4,)),
+            pltpu.SemaphoreType.DMA((5, rows)),
+            pltpu.SemaphoreType.DMA((5, planes)),
+            pltpu.SemaphoreType.DMA((5, planes)),
+            pltpu.SemaphoreType.DMA((5, rows)),
+            pltpu.SemaphoreType.DMA(pieces),
+            pltpu.SemaphoreType.DMA(pieces),
+            pltpu.SemaphoreType.DMA(pieces),
+            pltpu.SemaphoreType.DMA(pieces),
+            pltpu.SemaphoreType.REGULAR,
+            pltpu.SemaphoreType.REGULAR,
+            pltpu.SemaphoreType.DMA((5, rows)),
+            pltpu.SemaphoreType.DMA((5, rows)),
         ],
         compiler_params=pltpu.CompilerParams(
-            vmem_limit_bytes=63 << 20,
-            **({"collective_id": 0, "has_side_effects": True} if stages > 1 else {}),
+            vmem_limit_bytes=63 << 20, collective_id=0, has_side_effects=True
         ),
-    )(token_ids, order, timesteps, table, gain, bias, w_qkv, w_out, w_in, w_down)
+    )(tokens, table, norm_shard, w_qkv, w_out, w_in, w_down)
 
 
 def body(token_ids, order, timesteps, table, norm_gain, norm_bias, w_qkv, w_out, w_in, w_down):
-    stages = lax.axis_size("section")
-    vocab = table.shape[0]
-    bf16, f32 = jnp.bfloat16, jnp.float32
-    gathered = (
-        lax.all_gather(norm_gain[0].astype(bf16), "dp", axis=1, tiled=True).astype(f32),
-        lax.all_gather(norm_bias[0].astype(bf16), "dp", axis=1, tiled=True).astype(f32),
-        lax.all_gather(w_qkv[0].astype(bf16), "dp", axis=0, tiled=True),
-        lax.all_gather(w_out[0].astype(bf16), "dp", axis=0, tiled=True),
-        lax.all_gather(w_in[0].astype(bf16), "dp", axis=0, tiled=True),
-        lax.all_gather(w_down[0].astype(bf16), "dp", axis=0, tiled=True),
+    stages, planes = lax.axis_size("section"), lax.axis_size("dp")
+    vocab, width = table.shape
+    rows = planes // 2
+    stamps = jnp.broadcast_to(timesteps[:, :, None], token_ids.shape)
+    tokens = jnp.concatenate([token_ids, order, stamps], axis=1)
+    share = norm_gain.shape[2]
+    at_column = lax.axis_index("dp") * share
+    norm_shard = jnp.zeros((rows * NORM_ROWS, width), jnp.float32)
+    for kind, value in enumerate((norm_gain, norm_bias)):
+        norm_shard = lax.dynamic_update_slice(
+            norm_shard, value[0], (kind * NORM_ROWS, at_column)
+        )
+    sums = run_pipeline(stages, planes, tokens, table, norm_shard, w_qkv, w_out, w_in, w_down)
+    table_total = lax.psum(sums[0][:vocab], ("section", "dp"))
+    columns = width // stages
+    table_part = lax.dynamic_slice_in_dim(
+        table_total, lax.axis_index("section") * columns, columns, 1
     )
-    sums = run_pipeline(stages, token_ids, order, timesteps[:, :, None], table, gathered)
-    shared = [
-        lax.psum_scatter(value.astype(bf16), "dp", scatter_dimension=axis, tiled=True)
-        .astype(f32)[None]
-        for value, axis in zip(sums[1:7], (1, 1, 0, 0, 0, 0))
-    ]
-    table_part = lax.psum_scatter(
-        sums[0][:vocab].astype(bf16), "section", scatter_dimension=1, tiled=True
-    ).astype(f32)
-    return (lax.psum(table_part, "dp"), *shared)
+    norm_part = lax.dynamic_slice_in_dim(sums[1], at_column, share, 1)
+    return (
+        table_part,
+        norm_part[None, :2],
+        norm_part[None, NORM_ROWS : NORM_ROWS + 2],
+        *(total.astype(jnp.float32)[None] for total in sums[2:6]),
+    )
 
 
 def solution(mesh):

time: 602 us -> 424 us (0.70)
  waiting for transfers between devices: 291 us -> 0 us
  Pallas kernels: 209 us -> 373 us
  other arithmetic: 28.3 us -> 9.2 us
  blocking collectives: 51.8 us -> 34.3 us
  between operations: 14.3 us -> 0.67 us
    pallas_call x1, Pallas kernels: 209 us -> 373 us  [run_pipeline(): pl.pallas_call(functools.partial(pipeline_kernel, stages, planes), out_sh...]
    reduce_scatter x4 -> x0, waiting for transfers between devices: 129 us -> none  [body(): lax.psum_scatter(value.astype(bf16), 'dp', scatter_dimension=axis, tiled=...]
    all_gather x3 -> x0, waiting for transfers between devices: 103 us -> none  [the longest x1 47.1 us: body(): lax.all_gather(w_in[0].astype(bf16), 'dp', axis=0, tiled=True)]
    unnamed x13 -> x0, waiting for transfers between devices: 58.9 us -> none
    all_gather x3 -> x0, blocking collectives: 35.5 us -> none  [the longest x1 19.7 us: body(): lax.all_gather(w_out[0].astype(bf16), 'dp', axis=0, tiled=True)]
    convert_element_type x14 -> x0, other arithmetic: 19.3 us -> none  [the longest x6 14.3 us: body(): value.astype(bf16)]
    psum x1, blocking collectives: 16.3 us -> 34.3 us  [body(): table_total = lax.psum(sums[0][:vocab], ('section', 'dp'))]
  transfers between devices with their start and end apart: 10 -> 0, of which waited for: 10 -> 0; matrix products, arithmetic and copies ran while one was open for 5% -> 0% of each run, Pallas kernels for 0% -> 0%
where the time goes in v2:
time: 424 us; the launch traced here: 421 us
  Pallas kernels  373 us (88%)
  blocking collectives  34.3 us (8%)
  other arithmetic  9.2 us (2%)
    pallas_call x1, Pallas kernels, run_pipeline(): pl.pallas_call(functools.partial(pipeline_kernel, stages, planes), out_sh...  373 us
    psum x1, blocking collectives, body(): table_total = lax.psum(sums[0][:vocab], ('section', 'dp'))  34.3 us

profile of v2, /device:TPU:1, one launch (start us, length us, event | category | flops | bytes accessed | tf_op | source)
XLA Modules:
  0.0 420.8 jit_solution(8643009913979767221)
XLA Ops:
  0.6 0.7 bitcast_dynamic-update-slice_fusion.1
  1.3 0.7 bitcast_dynamic-update-slice_fusion.norm_shard
  2.0 0.0 copy-start
  2.0 0.7 broadcast_in_dim.42
  2.8 1.4 pad_add_fusion.token_in_ref
  4.1 0.0 copy-done
  4.1 372.6 %shard_map.153 = (f32[32,512]{1,0:T(8,128)}, f32[16,512]{1,0:T(8,128)}, bf16[128,1536]{1,0:T(8,128)(2,1)}, bf16[128,512]{1,0:T(8,128)(2,1)}, bf16[128,2048]{1,0:...) custom-call(s32[8,3,256]{2,1,0:T(4,128)} %pad_add_fusion.token_in_ref, f32[28,512]{1,0:T(8,128)} %table_ref.1, ...), custom_call_target="tpu_custom_call" | custom-call | tf_op jit(solution)/shard_map/pallas_call | solution.py:816
  376.7 1.3 dynamic-slice_bitcast_fusion
  378.0 34.3 %psum.7 = f32[28,512]{1,0:T(8,128)S(1)} all-reduce(f32[28,512]{1,0:T(8,128)} %bitcast.22), channel_id=1, replica_groups=mesh['section'=8,'dp'=4] {'section','dp'}, use_global_device_ids=true, to_apply=%region_0.0 | all-reduce | flops 14336 | bytes 114688 | tf_op jit(solution)/shard_map/psum | solution.py:886
  412.3 0.7 constant_dynamic-slice_fusion
  413.0 2.1 bitcast_convert_fusion
  415.1 2.1 bitcast_convert_fusion.1
  417.3 2.0 bitcast_convert_fusion.2
  419.2 1.6 bitcast_convert_fusion.3
  (1 shorter events, 0.0 us)
Async XLA Ops:
  2.0 2.1 copy-start

commit v3 on v2

--- a/solution.py
+++ b/solution.py
@@ -12,6 +12,7 @@
 EPSILON = 1e-05
 EMBED_GAIN = 16.0
 FF_CHUNK = 512
+AHEAD = 2
 NORM_ROWS = 8
 MESH = pl.DeviceIdType.MESH
 
@@ -144,12 +145,16 @@
     peer_free,
     total_send,
     total_recv,
+    table_slots,
+    table_send,
+    table_recv,
 ):
     micro_count, _, length = token_ref.shape
     vocab, width = table_ref.shape
     hidden_units = w_in_ref.shape[1]
     head_size = width // HEADS
     score_scale = 1.0 / math.sqrt(head_size)
+    root = math.sqrt(2.0 / math.pi)
     pair_width = 2 * head_size
     bf16, f32 = jnp.bfloat16, jnp.float32
 
@@ -226,6 +231,8 @@
         greet(owner)
         greet((stage, 2 * at_row + core))
         greet(peer(at_row))
+    for at_place in range(per_plane):
+        greet((2 * chip_of(at_place, row, per_plane) + core, plane))
     greet(partner)
     greet(ahead, stage < last)
     greet(behind, stage > 0)
@@ -439,9 +446,11 @@
         shown = jnp.where(visible, rows_of[0:1], vocab - 1)
         return (letters == shown).astype(bf16)
 
-    def halves(pair):
+    def stacked(pair):
         zero = jnp.zeros_like(pair)
-        return jnp.where(lower, pair, zero), jnp.where(lower, zero, pair)
+        return jnp.concatenate(
+            [jnp.where(lower, pair, zero), jnp.where(lower, zero, pair)], axis=0
+        )
 
     def load_hidden(micro):
         @pl.when(stage == 0)
@@ -488,23 +497,32 @@
         unit, _ = unit_rows(hidden)
         normed = (unit * gain_ref[0:1, :] + bias_ref[0:1, :]).astype(bf16)
         packed[micro] = dot(normed, w_qkv_ref[...], 1, 0).astype(bf16)
-        for pair in range(HEADS // 2):
+        pairs = HEADS // 2
+
+        def block(member, pair):
+            at = member * width + pair * pair_width
+            return packed[micro, :, at : at + pair_width]
+
+        def scores_of(pair):
+            query = block(0, pair) * jnp.asarray(score_scale, bf16)
+            return dot(stacked(query), block(1, pair), 1, 1)
+
+        waiting = [scores_of(pair) for pair in range(AHEAD)]
+        for pair in range(pairs):
+            if pair + AHEAD < pairs:
+                waiting.append(scores_of(pair + AHEAD))
+            scores = waiting[pair]
+            largest = jnp.max(scores, axis=-1, keepdims=True)
+            powers = jnp.exp(scores - largest)
+            total = jnp.sum(powers, axis=-1, keepdims=True)
+            attention = (powers * (1.0 / total)).astype(bf16)
+            attention_out[2 * pair] = attention[:length]
+            attention_out[2 * pair + 1] = attention[length:]
+            found = dot(attention, block(2, pair), 1, 0)
             at = pair * pair_width
-            query = packed[micro, :, at : at + pair_width] * jnp.asarray(score_scale, bf16)
-            key = packed[micro, :, width + at : width + at + pair_width]
-            value = packed[micro, :, 2 * width + at : 2 * width + at + pair_width]
-            found = []
-            for side, part in enumerate(halves(query)):
-                scores = dot(part, key, 1, 1)
-                largest = jnp.max(scores, axis=-1, keepdims=True)
-                powers = jnp.exp(scores - largest)
-                total = jnp.sum(powers, axis=-1, keepdims=True)
-                attention = (powers * (1.0 / total)).astype(bf16)
-                attention_out[2 * pair + side] = attention
-                found.append(dot(attention, value, 1, 0))
-            mixed[micro, :, at : at + pair_width] = jnp.where(lower, found[0], found[1]).astype(
-                bf16
-            )
+            mixed[micro, :, at : at + pair_width] = jnp.where(
+                lower, found[:length], found[length:]
+            ).astype(bf16)
         save = pltpu.make_async_copy(attention_out, stash_ref.at[micro], stash_sem)
         save.start()
         between = hidden + dot(mixed[micro], w_out_ref[...], 1, 0)
@@ -516,14 +534,12 @@
         normed_two = (unit * gain_ref[1:2, :] + bias_ref[1:2, :]).astype(bf16)
         for at in range(0, hidden_units, FF_CHUNK):
             lifted = dot(normed_two, w_in_ref[:, at : at + FF_CHUNK], 1, 0)
-            square = lifted * lifted
-            inner = math.sqrt(2.0 / math.pi) * lifted * (1.0 + 0.044715 * square)
-            bend = jnp.tanh(inner)
-            half = 0.5 * (1.0 + bend)
-            active[micro, :, at : at + FF_CHUNK] = (lifted * half).astype(bf16)
-            steep = math.sqrt(2.0 / math.pi) * (1.0 + 3.0 * 0.044715 * square)
+            bent = (root * 0.044715) * (lifted * lifted)
+            half = 0.5 + 0.5 * jnp.tanh(lifted * (bent + root))
+            gelu = lifted * half
+            active[micro, :, at : at + FF_CHUNK] = gelu.astype(bf16)
             slope[micro, :, at : at + FF_CHUNK] = (
-                half + 0.5 * lifted * (1.0 - bend * bend) * steep
+                half + gelu * ((1.0 - half) * (6.0 * bent + 2.0 * root))
             ).astype(bf16)
         if stages > 1:
             @pl.when(jnp.logical_and(micro >= 2, stage < last))
@@ -582,33 +598,37 @@
         g_mixed = dot(g_attended, w_out_ref[...], 1, 1).astype(bf16)
         load_hidden(micro)
         load.wait()
-        for pair in range(HEADS // 2):
+        pairs = HEADS // 2
+
+        def block(member, pair):
+            at = member * width + pair * pair_width
+            return packed[micro, :, at : at + pair_width]
+
+        def put(member, pair, value):
+            at = member * width + pair * pair_width
+            packed[micro, :, at : at + pair_width] = value.astype(bf16)
+
+        def g_attention_of(pair):
             at = pair * pair_width
-            query = packed[micro, :, at : at + pair_width]
-            key = packed[micro, :, width + at : width + at + pair_width]
-            value = packed[micro, :, 2 * width + at : 2 * width + at + pair_width]
-            g_pair = g_mixed[:, at : at + pair_width]
-            found = []
-            for side, part in enumerate(halves(g_pair)):
-                low = attention_in[2 * pair + side]
-                attention = low.astype(f32)
-                g_attention = dot(part, value, 1, 1)
-                inner = jnp.sum(attention * g_attention, axis=-1, keepdims=True)
-                g_scores = (attention * (g_attention - inner)).astype(bf16)
-                found.append(
-                    (
-                        dot(g_scores, key, 1, 0),
-                        dot(g_scores, query, 0, 0),
-                        dot(low, g_pair, 0, 0),
-                    )
-                )
-            for member, factor in enumerate((score_scale, score_scale, None)):
-                joined = jnp.where(lower, found[0][member], found[1][member])
-                if factor is not None:
-                    joined = joined * factor
-                packed[
-                    micro, :, member * width + at : member * width + at + pair_width
-                ] = joined.astype(bf16)
+            g_pair = stacked(g_mixed[:, at : at + pair_width])
+            return g_pair, dot(g_pair, block(2, pair), 1, 1)
+
+        waiting = [g_attention_of(pair) for pair in range(AHEAD)]
+        for pair in range(pairs):
+            if pair + AHEAD < pairs:
+                waiting.append(g_attention_of(pair + AHEAD))
+            g_pair, g_attention = waiting[pair]
+            low = attention_in[2 * pair : 2 * pair + 2].reshape(2 * length, length)
+            attention = low.astype(f32)
+            inner = jnp.sum(attention * g_attention, axis=-1, keepdims=True)
+            g_scores = (attention * (g_attention - inner)).astype(bf16)
+            key, query = block(1, pair), stacked(block(0, pair))
+            g_values = dot(low, g_pair, 0, 0)
+            g_queries = dot(g_scores, key, 1, 0)
+            g_keys = dot(g_scores, query, 0, 0)
+            put(0, pair, jnp.where(lower, g_queries[:length], g_queries[length:]) * score_scale)
+            put(1, pair, g_keys * score_scale)
+            put(2, pair, g_values)
         g_normed = dot(packed[micro], w_qkv_ref[...], 1, 1)
         unit, scale = unit_rows(work[...])
         h_in[micro] = (unit * gain_ref[0:1, :] + bias_ref[0:1, :]).astype(bf16)
@@ -672,7 +692,95 @@
             def _():
                 gradient_copy(micro, behind).wait_send()
 
-    d_table_ref[...] = table_sum[...]
+    def table_copy(source, target, send, recv, device):
+        return remote_copy(source, target, table_send.at[send], table_recv.at[recv], device)
+
+    def lane_copy():
+        return table_copy(table_sum, table_slots.at[0], 0, 0, (section, 0))
+
+    def table_core_copy():
+        return table_copy(table_sum, table_slots.at[1], 1, 1, partner)
+
+    def table_peer_copy(from_row, to_row):
+        return table_copy(
+            table_sum, table_slots.at[2 + from_row], 2 + to_row, 2 + from_row, peer(to_row)
+        )
+
+    def table_down_copy(to_plane):
+        return table_copy(
+            d_table_ref, d_table_ref, 2 + rows + to_plane, 2 + rows, (section, to_plane)
+        )
+
+    def table_side_copy(to_place):
+        target = 2 * chip_of(to_place, row, per_plane) + core
+        return table_copy(
+            d_table_ref, d_table_ref, 2 + rows + planes + to_place, 2 + rows, (target, plane)
+        )
+
+    @pl.when(stage == last)
+    def _():
+        lane_copy().start()
+
+    def table_cores():
+        @pl.when(stage == 0)
+        def _():
+            lane_copy().wait_recv()
+            table_sum[...] += table_slots[0]
+            table_core_copy().start()
+
+    def table_peers():
+        @pl.when(stage == 0)
+        def _():
+            table_core_copy().wait()
+            table_sum[...] += table_slots[1]
+            for to_row in range(rows):
+                @pl.when(to_row != row)
+                def _():
+                    table_peer_copy(row, to_row).start()
+
+    def table_side():
+        for to_place in range(1, per_plane):
+            table_side_copy(to_place).start()
+
+    def table_down():
+        @pl.when(stage == 0)
+        def _():
+            total = table_sum[...]
+            for from_row in range(rows):
+                @pl.when(from_row != row)
+                def _():
+                    table_peer_copy(from_row, from_row).wait_recv()
+
+                total = total + jnp.where(from_row != row, table_slots[2 + from_row], 0.0)
+            d_table_ref[...] = total
+            for to_plane in range(1, planes):
+                table_down_copy(to_plane).start()
+            table_side()
+
+    def table_done():
+        @pl.when(place > 0)
+        def _():
+            table_side_copy(0).wait_recv()
+
+        @pl.when(stage == last)
+        def _():
+            lane_copy().wait_send()
+
+        @pl.when(stage == 0)
+        def _():
+            for to_row in range(rows):
+                @pl.when(to_row != row)
+                def _():
+                    table_peer_copy(row, to_row).wait_send()
+
+            for to_plane in range(1, planes):
+                table_down_copy(to_plane).wait_send()
+
+        @pl.when(place == 0)
+        def _():
+            for to_place in range(1, per_plane):
+                table_side_copy(to_place).wait_send()
+
     for kind in range(2):
         totals = [
             jnp.sum(norm_sums[2 * kind + member], axis=0, keepdims=True) for member in range(2)
@@ -780,17 +888,27 @@
             wait_sent(*total_args(matrix, pair), here)
 
     order = (norms, 3, 2, 0, 1)
+    table_cores()
     pl.semaphore_wait(core_free, 1)
     for matrix in order:
         give_core(matrix)
+    table_peers()
     pl.semaphore_wait(peer_free, rows - 1)
     for position in range(count + 1):
         if position < count:
             give_peers(order[position])
         if position > 0:
             give_totals(order[position - 1])
+        if position == 1:
+            table_down()
+    @pl.when(jnp.logical_and(place == 0, plane > 0))
+    def _():
+        table_down_copy(0).wait_recv()
+        table_side()
+
     for matrix in order:
         finish(matrix)
+    table_done()
 
 
 def run_pipeline(stages, planes, tokens, table, norm_shard, w_qkv, w_out, w_in, w_down):
@@ -862,6 +980,9 @@
             pltpu.SemaphoreType.REGULAR,
             pltpu.SemaphoreType.DMA((5, rows)),
             pltpu.SemaphoreType.DMA((5, rows)),
+            pltpu.VMEM((2 + rows, table_rows, width), f32),
+            pltpu.SemaphoreType.DMA((2 + rows + planes + stages // planes,)),
+            pltpu.SemaphoreType.DMA((3 + rows,)),
         ],
         compiler_params=pltpu.CompilerParams(
             vmem_limit_bytes=63 << 20, collective_id=0, has_side_effects=True
@@ -883,10 +1004,9 @@
             norm_shard, value[0], (kind * NORM_ROWS, at_column)
         )
     sums = run_pipeline(stages, planes, tokens, table, norm_shard, w_qkv, w_out, w_in, w_down)
-    table_total = lax.psum(sums[0][:vocab], ("section", "dp"))
     columns = width // stages
-    table_part = lax.dynamic_slice_in_dim(
-        table_total, lax.axis_index("section") * columns, columns, 1
+    table_part = lax.dynamic_slice(
+        sums[0], (0, lax.axis_index("section") * columns), (vocab, columns)
     )
     norm_part = lax.dynamic_slice_in_dim(sums[1], at_column, share, 1)
     return (

time: 424 us -> 361 us (0.85)
  blocking collectives: 34.3 us -> 0 us
  Pallas kernels: 373 us -> 346 us
    psum x1 -> x0, blocking collectives: 34.3 us -> none  [body(): table_total = lax.psum(sums[0][:vocab], ('section', 'dp'))]
    pallas_call x1, Pallas kernels: 373 us -> 346 us  [run_pipeline(): pl.pallas_call(functools.partial(pipeline_kernel, stages, planes), out_sh...]
where the time goes in v3:
time: 361 us
  Pallas kernels  346 us (96%)
  other arithmetic  9.2 us (3%)
  local copies, waits for them, and re-layouts  4.78 us (1%)
    pallas_call x1, Pallas kernels, run_pipeline(): pl.pallas_call(functools.partial(pipeline_kernel, stages, planes), out_sh...  346 us
    broadcast_in_dim x4, other arithmetic, body(): total.astype(jnp.float32)[None]  7.84 us

profile of v3, /device:TPU:1, one launch (start us, length us, event | category | flops | bytes accessed | tf_op | source)
XLA Modules:
  0.0 360.7 jit_solution(6957212674112146674)
XLA Ops:
  0.6 0.7 bitcast_dynamic-update-slice_fusion.1
  1.3 0.7 bitcast_dynamic-update-slice_fusion.norm_shard
  2.0 0.0 copy-start
  2.0 0.7 broadcast_in_dim.42
  2.8 1.4 pad_add_fusion.token_in_ref
  4.1 0.0 copy-done
  4.1 346.1 %shard_map.153 = (f32[32,512]{1,0:T(8,128)}, f32[16,512]{1,0:T(8,128)}, bf16[128,1536]{1,0:T(8,128)(2,1)}, bf16[128,512]{1,0:T(8,128)(2,1)}, bf16[128,2048]{1,0:...) custom-call(s32[8,3,256]{2,1,0:T(4,128)} %pad_add_fusion.token_in_ref, f32[28,512]{1,0:T(8,128)} %table_ref.1, ...), custom_call_target="tpu_custom_call" | custom-call | tf_op jit(solution)/shard_map/pallas_call | solution.py:934
  350.2 1.3 dynamic-slice_bitcast_fusion
  351.5 1.4 constant_dynamic-slice_fusion
  352.9 2.1 bitcast_convert_fusion
  355.0 2.1 bitcast_convert_fusion.1
  357.1 2.0 bitcast_convert_fusion.2
  359.1 1.6 bitcast_convert_fusion.3
  (1 shorter events, 0.0 us)
Async XLA Ops:
  2.0 2.1 copy-start

commit v4 on v3

--- a/solution.py
+++ b/solution.py
@@ -82,9 +82,12 @@
 def pipeline_kernel(
     stages,
     planes,
-    token_in_ref,
+    ids_ref,
+    order_ref,
+    stamp_ref,
     table_ref,
-    norm_shard,
+    gain_shard,
+    bias_shard,
     qkv_shard,
     out_shard,
     in_shard,
@@ -96,6 +99,8 @@
     in_total,
     down_total,
     stash_ref,
+    token_in_ref,
+    norm_shard,
     token_ref,
     h_in,
     g_in,
@@ -205,6 +210,18 @@
     home_plane = lax.div(section, per_plane)
     carries = lax.rem(plane, 2) == core
 
+    for micro in range(micro_count):
+        token_in_ref[micro, 0:1, :] = ids_ref[micro]
+        token_in_ref[micro, 1:2, :] = order_ref[micro]
+        token_in_ref[micro, 2:3, :] = jnp.broadcast_to(stamp_ref[micro : micro + 1, :], (1, length))
+    norm_shard[...] = jnp.zeros_like(norm_shard)
+    share = gain_shard.shape[2]
+    columns = lax.broadcasted_iota(jnp.int32, (2, width), 1)
+    mine = jnp.logical_and(columns >= plane * share, columns < (plane + 1) * share)
+    for kind, shard in enumerate((gain_shard, bias_shard)):
+        spread_out = jnp.concatenate([shard[0]] * planes, axis=1)
+        norm_shard[kind * NORM_ROWS : kind * NORM_ROWS + 2, :] = jnp.where(mine, spread_out, 0.0)
+
     barrier = pltpu.get_barrier_semaphore()
     greetings = []
 
@@ -238,16 +255,23 @@
     greet(behind, stage > 0)
     pl.semaphore_wait(barrier, sum(greetings))
 
-    matrices = (
-        (w_qkv_ref, d_qkv_ref, qkv_shard, qkv_total, packed),
-        (w_out_ref, d_out_ref, out_shard, out_total, mixed),
-        (w_in_ref, d_in_ref, in_shard, in_total, active),
-        (w_down_ref, d_down_ref, down_shard, down_total, middle),
-        (norm_full, d_norm_ref, norm_shard, norm_total, norm_slots),
-    )
+    matrices = []
+    for parts, *members in (
+        (2, w_qkv_ref, d_qkv_ref, qkv_shard, qkv_total, packed),
+        (1, w_out_ref, d_out_ref, out_shard, out_total, mixed),
+        (2, w_in_ref, d_in_ref, in_shard, in_total, active),
+        (2, w_down_ref, d_down_ref, down_shard, down_total, middle),
+        (1, norm_full, d_norm_ref, norm_shard, norm_total, norm_slots),
+    ):
+        window = members[0].shape[1] // parts
+        for part in range(parts):
+            matrices.append((*members, pl.ds(part * window, window)))
     count = len(matrices)
     norms = count - 1
     heights = [matrix[0].shape[0] // (planes * rows) for matrix in matrices]
+
+    def view(matrix, member, rows_of):
+        return matrices[matrix][member].at[rows_of, matrices[matrix][5]]
 
     def slot(matrix, index):
         buffer, height = matrices[matrix][4], heights[matrix]
@@ -257,7 +281,7 @@
             inside = pl.multiple_of(inside * height, height)
         else:
             inside = inside * height
-        return buffer.at[block, pl.ds(inside, height)]
+        return buffer.at[block, pl.ds(inside, height), matrices[matrix][5]]
 
     def piece(matrix, quarter, at_row):
         height = heights[matrix]
@@ -282,10 +306,12 @@
 
     loads = []
     for matrix in range(norms):
-        shard, landing = matrices[matrix][2], matrices[matrix][1]
+        shard, window = matrices[matrix][2], matrices[matrix][5]
         loads.append(
             pltpu.make_async_copy(
-                shard.at[0], landing.at[pl.ds(0, shard.shape[1])], load_sem.at[matrix]
+                shard.at[0, :, window],
+                view(matrix, 1, pl.ds(0, shard.shape[1])),
+                load_sem.at[matrix],
             )
         )
         loads[-1].start()
@@ -307,14 +333,14 @@
     def plane_args(matrix, to_plane, from_plane):
         return (
             slot(matrix, to_plane),
-            matrices[matrix][0].at[piece(matrix, from_plane, row)],
+            view(matrix, 0, piece(matrix, from_plane, row)),
             plane_send.at[matrix, to_plane],
             plane_recv.at[matrix, lax.div(from_plane, 2)],
             (section, to_plane),
         )
 
     def peer_args(matrix, quarter_pair, from_row, to_row):
-        part = matrices[matrix][0].at[piece(matrix, 2 * quarter_pair + core, from_row)]
+        part = view(matrix, 0, piece(matrix, 2 * quarter_pair + core, from_row))
         return (
             part,
             part,
@@ -324,7 +350,7 @@
         )
 
     def core_args(matrix, quarter_pair, at_row, from_core):
-        part = matrices[matrix][0].at[piece(matrix, 2 * quarter_pair + from_core, at_row)]
+        part = view(matrix, 0, piece(matrix, 2 * quarter_pair + from_core, at_row))
         return (
             part,
             part,
@@ -338,8 +364,8 @@
             loads[matrix].wait()
             for at_row in range(rows):
                 height = heights[matrix]
-                source = matrices[matrix][1][at_row * height : (at_row + 1) * height, :]
-                slot(matrix, planes + at_row)[...] = source.astype(bf16)
+                source = view(matrix, 1, pl.ds(at_row * height, height))
+                slot(matrix, planes + at_row)[...] = source[...].astype(bf16)
         for at_row in range(rows):
             start_copy(*spread_args(matrix, at_row), here)
 
@@ -397,7 +423,7 @@
                 remote_copy(*core_args(matrix, pair, at_row, core)).wait_send()
 
     steps_of_gather = (spread, along_planes, between_peers, between_cores, gathered)
-    order = (norms, 0, 1, 2, 3)
+    order = (norms, *range(norms))
     for turn_at in range(count + len(steps_of_gather) - 1):
         for depth, action in enumerate(steps_of_gather):
             if 0 <= turn_at - depth < count:
@@ -824,7 +850,7 @@
         height = heights[matrix]
         return (
             slot(matrix, 2 * rows * rows + pair * rows + row),
-            matrices[matrix][3].at[pl.ds(pl.multiple_of(row * height, height), height)],
+            view(matrix, 3, pl.ds(pl.multiple_of(row * height, height), height)),
             total_send.at[matrix, pair],
             total_recv.at[matrix, row],
             (stage, 2 * pair + core),
@@ -834,8 +860,8 @@
         for pair in range(rows):
             for at_row in range(rows):
                 args = core_sum_args(matrix, pair, at_row)
-                part = matrices[matrix][1][piece(matrix, 2 * pair + 1 - core, at_row), :]
-                args[0][...] = part.astype(args[0].dtype)
+                part = view(matrix, 1, piece(matrix, 2 * pair + 1 - core, at_row))
+                args[0][...] = part[...].astype(args[0].dtype)
                 remote_copy(*args).start()
 
     def give_peers(matrix):
@@ -843,7 +869,7 @@
             for at_row in range(rows):
                 remote_copy(*core_sum_args(matrix, pair, at_row)).wait_recv()
                 landed = slot(matrix, rows * rows + pair * rows + at_row)
-                part = matrices[matrix][1].at[piece(matrix, 2 * pair + core, at_row)]
+                part = view(matrix, 1, piece(matrix, 2 * pair + core, at_row))
                 total = part[...] + landed[...].astype(f32)
 
                 @pl.when(at_row != row)
@@ -858,7 +884,7 @@
 
     def give_totals(matrix):
         for pair in range(rows):
-            part = matrices[matrix][1].at[piece(matrix, 2 * pair + core, row)]
+            part = view(matrix, 1, piece(matrix, 2 * pair + core, row))
             for from_row in range(rows):
                 @pl.when(from_row != row)
                 def _():
@@ -873,7 +899,7 @@
     def finish(matrix):
         height = heights[matrix]
         for from_row in range(rows):
-            part = matrices[matrix][3].at[pl.ds(from_row * height, height)]
+            part = view(matrix, 3, pl.ds(from_row * height, height))
             remote_copy(
                 part, part, total_send.at[matrix, 0], total_recv.at[matrix, from_row], partner
             ).wait_recv()
@@ -887,20 +913,22 @@
 
             wait_sent(*total_args(matrix, pair), here)
 
-    order = (norms, 3, 2, 0, 1)
+    order = tuple(reversed(range(count)))
     table_cores()
     pl.semaphore_wait(core_free, 1)
-    for matrix in order:
-        give_core(matrix)
-    table_peers()
-    pl.semaphore_wait(peer_free, rows - 1)
-    for position in range(count + 1):
+    for position in range(count + 3):
         if position < count:
-            give_peers(order[position])
-        if position > 0:
-            give_totals(order[position - 1])
+            give_core(order[position])
         if position == 1:
+            table_peers()
+            pl.semaphore_wait(peer_free, rows - 1)
+        if 0 <= position - 1 < count:
+            give_peers(order[position - 1])
+        if 0 <= position - 3 < count:
+            give_totals(order[position - 3])
+        if position == 4:
             table_down()
+
     @pl.when(jnp.logical_and(place == 0, plane > 0))
     def _():
         table_down_copy(0).wait_recv()
@@ -911,8 +939,9 @@
     table_done()
 
 
-def run_pipeline(stages, planes, tokens, table, norm_shard, w_qkv, w_out, w_in, w_down):
-    micro_count, _, length = tokens.shape
+def run_pipeline(stages, planes, token_ids, order, timesteps, table, gain, bias, *shards):
+    w_qkv, w_out, w_in, w_down = shards
+    micro_count, _, length = token_ids.shape
     width = table.shape[1]
     hidden_units = w_in.shape[2]
     rows = planes // 2
@@ -920,24 +949,28 @@
     bf16, f32 = jnp.bfloat16, jnp.float32
     vmem = pl.BlockSpec(memory_space=pltpu.VMEM)
     anywhere = pl.BlockSpec(memory_space=pl.ANY)
-    shards = (w_qkv, w_out, w_in, w_down)
+    tokens = (micro_count, 3, length)
+    norm_shard = (rows * NORM_ROWS, width)
     full = [(shard.shape[1] * planes, shard.shape[2]) for shard in shards]
-    norm_full = (planes * norm_shard.shape[0], width)
+    norm_full = (planes * rows * NORM_ROWS, width)
     outs = (
         jax.ShapeDtypeStruct((table_rows, width), f32),
-        jax.ShapeDtypeStruct(norm_shard.shape, f32),
+        jax.ShapeDtypeStruct(norm_shard, f32),
         *(jax.ShapeDtypeStruct(shard.shape[1:], bf16) for shard in shards),
         jax.ShapeDtypeStruct((micro_count, HEADS, length, length), bf16),
     )
     rows_shape = (micro_count, length, width)
-    pieces = (5, rows, rows)
+    units = 8
+    pieces = (units, rows, rows)
     return pl.pallas_call(
         functools.partial(pipeline_kernel, stages, planes),
         out_shape=outs,
-        in_specs=[vmem] * 3 + [anywhere] * 4,
+        in_specs=[vmem] * 6 + [anywhere] * 4,
         out_specs=[vmem] * 6 + [anywhere],
         scratch_shapes=[
-            pltpu.VMEM(tokens.shape, jnp.int32),
+            pltpu.VMEM(tokens, jnp.int32),
+            pltpu.VMEM(norm_shard, f32),
+            pltpu.VMEM(tokens, jnp.int32),
             pltpu.VMEM(rows_shape, bf16),
             pltpu.VMEM(rows_shape, bf16),
             pltpu.VMEM((2, length, width), bf16),
@@ -967,19 +1000,19 @@
             pltpu.SemaphoreType.DMA,
             pltpu.SemaphoreType.DMA((2,)),
             pltpu.SemaphoreType.DMA,
-            pltpu.SemaphoreType.DMA((4,)),
-            pltpu.SemaphoreType.DMA((5, rows)),
-            pltpu.SemaphoreType.DMA((5, planes)),
-            pltpu.SemaphoreType.DMA((5, planes)),
-            pltpu.SemaphoreType.DMA((5, rows)),
+            pltpu.SemaphoreType.DMA((units,)),
+            pltpu.SemaphoreType.DMA((units, rows)),
+            pltpu.SemaphoreType.DMA((units, planes)),
+            pltpu.SemaphoreType.DMA((units, planes)),
+            pltpu.SemaphoreType.DMA((units, rows)),
             pltpu.SemaphoreType.DMA(pieces),
             pltpu.SemaphoreType.DMA(pieces),
             pltpu.SemaphoreType.DMA(pieces),
             pltpu.SemaphoreType.DMA(pieces),
             pltpu.SemaphoreType.REGULAR,
             pltpu.SemaphoreType.REGULAR,
-            pltpu.SemaphoreType.DMA((5, rows)),
-            pltpu.SemaphoreType.DMA((5, rows)),
+            pltpu.SemaphoreType.DMA((units, rows)),
+            pltpu.SemaphoreType.DMA((units, rows)),
             pltpu.VMEM((2 + rows, table_rows, width), f32),
             pltpu.SemaphoreType.DMA((2 + rows + planes + stages // planes,)),
             pltpu.SemaphoreType.DMA((3 + rows,)),
@@ -987,34 +1020,83 @@
         compiler_params=pltpu.CompilerParams(
             vmem_limit_bytes=63 << 20, collective_id=0, has_side_effects=True
         ),
-    )(tokens, table, norm_shard, w_qkv, w_out, w_in, w_down)
+    )(token_ids, order, timesteps, table, gain, bias, w_qkv, w_out, w_in, w_down)
+
+
+def finish_kernel(planes, stages, *refs):
+    table_ref, norm_ref, *totals = refs[:6]
+    table_part, gain_part, bias_part, *results = refs[6:]
+    section, plane = lax.axis_index("section"), lax.axis_index("dp")
+    for total, result in zip(totals, results):
+        result[0] = total[...].astype(jnp.float32)
+
+    @pl.when(pl.program_id(0) == 0)
+    def _():
+        vocab, columns = table_part.shape
+        part = jnp.zeros((vocab, columns), jnp.float32)
+        for at in range(stages):
+            block = table_ref[:vocab, at * columns : (at + 1) * columns]
+            part = jnp.where(section == at, block, part)
+        table_part[...] = part
+        share = gain_part.shape[2]
+        for kind, result in enumerate((gain_part, bias_part)):
+            part = jnp.zeros((2, share), jnp.float32)
+            for at in range(planes):
+                start = kind * NORM_ROWS
+                block = norm_ref[start : start + 2, at * share : (at + 1) * share]
+                part = jnp.where(plane == at, block, part)
+            result[0] = part
+
+
+def run_finish(stages, planes, vocab, share, sums):
+    f32 = jnp.float32
+    steps = 4
+    whole = [pl.BlockSpec(value.shape, lambda i: (0, 0)) for value in sums[:2]]
+    blocks = [
+        pl.BlockSpec((value.shape[0] // steps, value.shape[1]), lambda i: (i, 0))
+        for value in sums[2:]
+    ]
+    out_blocks = [
+        pl.BlockSpec((1, value.shape[0] // steps, value.shape[1]), lambda i: (0, i, 0))
+        for value in sums[2:]
+    ]
+    columns = sums[0].shape[1] // stages
+    return pl.pallas_call(
+        functools.partial(finish_kernel, planes, stages),
+        grid=(steps,),
+        out_shape=(
+            jax.ShapeDtypeStruct((vocab, columns), f32),
+            jax.ShapeDtypeStruct((1, 2, share), f32),
+            jax.ShapeDtypeStruct((1, 2, share), f32),
+            *(jax.ShapeDtypeStruct((1, *value.shape), f32) for value in sums[2:]),
+        ),
+        in_specs=whole + blocks,
+        out_specs=[
+            pl.BlockSpec((vocab, columns), lambda i: (0, 0)),
+            pl.BlockSpec((1, 2, share), lambda i: (0, 0, 0)),
+            pl.BlockSpec((1, 2, share), lambda i: (0, 0, 0)),
+            *out_blocks,
+        ],
+    )(*sums)
 
 
 def body(token_ids, order, timesteps, table, norm_gain, norm_bias, w_qkv, w_out, w_in, w_down):
     stages, planes = lax.axis_size("section"), lax.axis_size("dp")
-    vocab, width = table.shape
-    rows = planes // 2
-    stamps = jnp.broadcast_to(timesteps[:, :, None], token_ids.shape)
-    tokens = jnp.concatenate([token_ids, order, stamps], axis=1)
-    share = norm_gain.shape[2]
-    at_column = lax.axis_index("dp") * share
-    norm_shard = jnp.zeros((rows * NORM_ROWS, width), jnp.float32)
-    for kind, value in enumerate((norm_gain, norm_bias)):
-        norm_shard = lax.dynamic_update_slice(
-            norm_shard, value[0], (kind * NORM_ROWS, at_column)
-        )
-    sums = run_pipeline(stages, planes, tokens, table, norm_shard, w_qkv, w_out, w_in, w_down)
-    columns = width // stages
-    table_part = lax.dynamic_slice(
-        sums[0], (0, lax.axis_index("section") * columns), (vocab, columns)
+    sums = run_pipeline(
+        stages,
+        planes,
+        token_ids,
+        order,
+        timesteps,
+        table,
+        norm_gain,
+        norm_bias,
+        w_qkv,
+        w_out,
+        w_in,
+        w_down,
     )
-    norm_part = lax.dynamic_slice_in_dim(sums[1], at_column, share, 1)
-    return (
-        table_part,
-        norm_part[None, :2],
-        norm_part[None, NORM_ROWS : NORM_ROWS + 2],
-        *(total.astype(jnp.float32)[None] for total in sums[2:6]),
-    )
+    return tuple(run_finish(stages, planes, table.shape[0], norm_gain.shape[2], sums[:6]))
 
 
 def solution(mesh):

time: 361 us -> 350 us (0.970)
  other arithmetic: 9.2 us -> 0 us
    broadcast_in_dim x4 -> x0, other arithmetic: 7.84 us -> none  [body(): total.astype(jnp.float32)[None]]
    pallas_call x0 -> x1, Pallas kernels: none -> 4.57 us  [run_finish(): pl.pallas_call(functools.partial(finish_kernel, planes, stages), grid=(st...]
where the time goes in v4:
time: 350 us
  Pallas kernels  347 us (99%)
    pallas_call x1, Pallas kernels, run_pipeline(): pl.pallas_call(functools.partial(pipeline_kernel, stages, planes), out_sh...  343 us

profile of v4, /device:TPU:1, one launch (start us, length us, event | category | flops | bytes accessed | tf_op | source)
XLA Modules:
  0.0 349.6 jit_solution(2006088972150431396)
XLA Ops:
  0.6 1.3 copy.17.stamp_ref
  2.0 342.9 %shard_map.153 = (f32[32,512]{1,0:T(8,128)}, f32[16,512]{1,0:T(8,128)}, bf16[128,1536]{1,0:T(8,128)(2,1)}, bf16[128,512]{1,0:T(8,128)(2,1)}, bf16[128,2048]{1,0:...) custom-call(s32[8,1,256]{2,1,0:T(1,128)} %ids_ref.1, s32[8,1,256]{2,1,0:T(1,128)} %order_ref.1, ...), custom_call_target="tpu_custom_call" | custom-call | tf_op jit(solution)/shard_map/pallas_call | solution.py:965
  344.9 4.6 %shard_map.154 = (f32[28,64]{1,0:T(8,128)}, f32[1,2,128]{2,1,0:T(2,128)}, f32[1,2,128]{2,1,0:T(2,128)}, f32[1,128,1536]{2,1,0:T(8,128)}, f32[1,128,512]{2,1,0:T(...) custom-call(f32[32,512]{1,0:T(8,128)} %get-tuple-element.13.refs_0_, f32[16,512]{1,0:T(8,128)} %get-tuple-element.14.refs_1_, ...), custom_call_target="tpu_custom_call" | custom-call | tf_op jit(solution)/shard_map/pallas_call | solution.py:1064

commit v5 on v4

--- a/solution.py
+++ b/solution.py
@@ -12,7 +12,8 @@
 EPSILON = 1e-05
 EMBED_GAIN = 16.0
 FF_CHUNK = 512
-AHEAD = 2
+AHEAD = 3
+WARM = 3
 NORM_ROWS = 8
 MESH = pl.DeviceIdType.MESH
 
@@ -111,8 +112,7 @@
     middle,
     active,
     slope,
-    attention_out,
-    attention_in,
+    attention_kept,
     work,
     table_parts,
     norm_sums,
@@ -125,7 +125,6 @@
     w_down_ref,
     gain_ref,
     bias_ref,
-    d_norm_ref,
     d_qkv_ref,
     d_out_ref,
     d_in_ref,
@@ -153,6 +152,12 @@
     table_slots,
     table_send,
     table_recv,
+    more_norm,
+    more_qkv,
+    more_out,
+    more_in,
+    more_down,
+    direct_recv,
 ):
     micro_count, _, length = token_ref.shape
     vocab, width = table_ref.shape
@@ -209,18 +214,6 @@
 
     home_plane = lax.div(section, per_plane)
     carries = lax.rem(plane, 2) == core
-
-    for micro in range(micro_count):
-        token_in_ref[micro, 0:1, :] = ids_ref[micro]
-        token_in_ref[micro, 1:2, :] = order_ref[micro]
-        token_in_ref[micro, 2:3, :] = jnp.broadcast_to(stamp_ref[micro : micro + 1, :], (1, length))
-    norm_shard[...] = jnp.zeros_like(norm_shard)
-    share = gain_shard.shape[2]
-    columns = lax.broadcasted_iota(jnp.int32, (2, width), 1)
-    mine = jnp.logical_and(columns >= plane * share, columns < (plane + 1) * share)
-    for kind, shard in enumerate((gain_shard, bias_shard)):
-        spread_out = jnp.concatenate([shard[0]] * planes, axis=1)
-        norm_shard[kind * NORM_ROWS : kind * NORM_ROWS + 2, :] = jnp.where(mine, spread_out, 0.0)
 
     barrier = pltpu.get_barrier_semaphore()
     greetings = []
@@ -253,15 +246,13 @@
     greet(partner)
     greet(ahead, stage < last)
     greet(behind, stage > 0)
-    pl.semaphore_wait(barrier, sum(greetings))
-
     matrices = []
     for parts, *members in (
-        (2, w_qkv_ref, d_qkv_ref, qkv_shard, qkv_total, packed),
-        (1, w_out_ref, d_out_ref, out_shard, out_total, mixed),
-        (2, w_in_ref, d_in_ref, in_shard, in_total, active),
-        (2, w_down_ref, d_down_ref, down_shard, down_total, middle),
-        (1, norm_full, d_norm_ref, norm_shard, norm_total, norm_slots),
+        (2, w_qkv_ref, d_qkv_ref, qkv_shard, qkv_total, packed, more_qkv),
+        (1, w_out_ref, d_out_ref, out_shard, out_total, mixed, more_out),
+        (2, w_in_ref, d_in_ref, in_shard, in_total, active, more_in),
+        (2, w_down_ref, d_down_ref, down_shard, down_total, middle, more_down),
+        (1, norm_full, norm_full, norm_shard, norm_total, norm_slots, more_norm),
     ):
         window = members[0].shape[1] // parts
         for part in range(parts):
@@ -271,7 +262,7 @@
     heights = [matrix[0].shape[0] // (planes * rows) for matrix in matrices]
 
     def view(matrix, member, rows_of):
-        return matrices[matrix][member].at[rows_of, matrices[matrix][5]]
+        return matrices[matrix][member].at[rows_of, matrices[matrix][-1]]
 
     def slot(matrix, index):
         buffer, height = matrices[matrix][4], heights[matrix]
@@ -281,11 +272,52 @@
             inside = pl.multiple_of(inside * height, height)
         else:
             inside = inside * height
-        return buffer.at[block, pl.ds(inside, height), matrices[matrix][5]]
+        return buffer.at[block, pl.ds(inside, height), matrices[matrix][-1]]
 
     def piece(matrix, quarter, at_row):
         height = heights[matrix]
         return pl.ds(pl.multiple_of((quarter * rows + at_row) * height, height), height)
+
+    loads = []
+    for matrix in range(norms):
+        shard, window = matrices[matrix][2], matrices[matrix][-1]
+        loads.append(
+            pltpu.make_async_copy(
+                shard.at[0, :, window],
+                view(matrix, 1, pl.ds(0, shard.shape[1])),
+                load_sem.at[matrix],
+            )
+        )
+        loads[-1].start()
+
+    for micro in range(micro_count):
+        token_in_ref[micro, 0:1, :] = ids_ref[micro]
+        token_in_ref[micro, 1:2, :] = order_ref[micro]
+        token_in_ref[micro, 2:3, :] = jnp.full((1, length), stamp_ref[micro, 0], jnp.int32)
+    norm_shard[...] = jnp.zeros_like(norm_shard)
+    share = gain_shard.shape[2]
+    columns = lax.broadcasted_iota(jnp.int32, (2, width), 1)
+    mine = jnp.logical_and(columns >= plane * share, columns < (plane + 1) * share)
+    for kind, shard in enumerate((gain_shard, bias_shard)):
+        spread_out = jnp.concatenate([shard[0]] * planes, axis=1)
+        norm_shard[kind * NORM_ROWS : kind * NORM_ROWS + 2, :] = jnp.where(mine, spread_out, 0.0)
+
+    table_rows = table_parts.shape[1]
+    work[:table_rows, :] = jnp.zeros((table_rows, width), f32)
+    work[:vocab, :] = table_ref[...]
+    rest = work[:table_rows, :]
+    for part in range(3):
+        rounded = rest.astype(bf16)
+        table_parts[part] = rounded
+        rest = rest - rounded.astype(f32)
+    norm_sums[...] = jnp.zeros_like(norm_sums)
+    table_sum[...] = jnp.zeros_like(table_sum)
+    for matrix in range(norms):
+        loads[matrix].wait()
+        for at_row in range(rows):
+            source = view(matrix, 1, pl.ds(at_row * heights[matrix], heights[matrix]))
+            slot(matrix, planes + at_row)[...] = source[...].astype(bf16)
+    pl.semaphore_wait(barrier, sum(greetings))
 
     gives_tokens = jnp.logical_and(place == 0, lane_index == plane)
     takes_tokens = jnp.logical_or(stage == 0, stage == last)
@@ -303,18 +335,6 @@
     def _():
         for index, target in enumerate((0, planes - 1)):
             start_copy(*token_copy(index, target), here)
-
-    loads = []
-    for matrix in range(norms):
-        shard, window = matrices[matrix][2], matrices[matrix][5]
-        loads.append(
-            pltpu.make_async_copy(
-                shard.at[0, :, window],
-                view(matrix, 1, pl.ds(0, shard.shape[1])),
-                load_sem.at[matrix],
-            )
-        )
-        loads[-1].start()
 
     def spread_args(matrix, at_row):
         target, _ = layer_device(section, at_row, lax.rem(plane, 2))
@@ -360,12 +380,6 @@
         )
 
     def spread(matrix):
-        if matrix != norms:
-            loads[matrix].wait()
-            for at_row in range(rows):
-                height = heights[matrix]
-                source = view(matrix, 1, pl.ds(at_row * height, height))
-                slot(matrix, planes + at_row)[...] = source[...].astype(bf16)
         for at_row in range(rows):
             start_copy(*spread_args(matrix, at_row), here)
 
@@ -428,6 +442,9 @@
         for depth, action in enumerate(steps_of_gather):
             if 0 <= turn_at - depth < count:
                 action(order[turn_at - depth])
+        if 1 <= turn_at <= 4:
+            sums = (d_qkv_ref, d_out_ref, d_in_ref, d_down_ref)[turn_at - 1]
+            sums[...] = jnp.zeros_like(sums)
     for matrix in range(count):
         gather_sent(matrix)
 
@@ -446,21 +463,6 @@
             start = (quarter * rows + kind) * NORM_ROWS
             total = total + norm_full[start : start + NORM_ROWS, :]
         ref[...] = total.astype(bf16).astype(f32)
-
-    table_rows = table_parts.shape[1]
-    work[:table_rows, :] = jnp.zeros((table_rows, width), f32)
-    work[:vocab, :] = table_ref[...]
-    rest = work[:table_rows, :]
-    for part in range(3):
-        rounded = rest.astype(bf16)
-        table_parts[part] = rounded
-        rest = rest - rounded.astype(f32)
-    d_qkv_ref[...] = jnp.zeros_like(d_qkv_ref)
-    d_out_ref[...] = jnp.zeros_like(d_out_ref)
-    d_in_ref[...] = jnp.zeros_like(d_in_ref)
-    d_down_ref[...] = jnp.zeros_like(d_down_ref)
-    norm_sums[...] = jnp.zeros_like(norm_sums)
-    table_sum[...] = jnp.zeros_like(table_sum)
 
     letters = lax.broadcasted_iota(jnp.int32, (table_rows, length), 0)
     lane = lax.broadcasted_iota(jnp.int32, (length, pair_width), 1)
@@ -542,14 +544,14 @@
             powers = jnp.exp(scores - largest)
             total = jnp.sum(powers, axis=-1, keepdims=True)
             attention = (powers * (1.0 / total)).astype(bf16)
-            attention_out[2 * pair] = attention[:length]
-            attention_out[2 * pair + 1] = attention[length:]
+            attention_kept[2 * pair] = attention[:length]
+            attention_kept[2 * pair + 1] = attention[length:]
             found = dot(attention, block(2, pair), 1, 0)
             at = pair * pair_width
             mixed[micro, :, at : at + pair_width] = jnp.where(
                 lower, found[:length], found[length:]
             ).astype(bf16)
-        save = pltpu.make_async_copy(attention_out, stash_ref.at[micro], stash_sem)
+        save = pltpu.make_async_copy(attention_kept, stash_ref.at[micro], stash_sem)
         save.start()
         between = hidden + dot(mixed[micro], w_out_ref[...], 1, 0)
         high = between.astype(bf16)
@@ -605,7 +607,7 @@
             @pl.when(stage < last)
             def _():
                 gradient_copy(micro, ahead).wait_recv()
-        load = pltpu.make_async_copy(stash_ref.at[micro], attention_in, stash_sem)
+        load = pltpu.make_async_copy(stash_ref.at[micro], attention_kept, stash_sem)
         load.start()
         g_out = g_in[micro]
         for at in range(0, hidden_units, FF_CHUNK):
@@ -644,7 +646,7 @@
             if pair + AHEAD < pairs:
                 waiting.append(g_attention_of(pair + AHEAD))
             g_pair, g_attention = waiting[pair]
-            low = attention_in[2 * pair : 2 * pair + 2].reshape(2 * length, length)
+            low = attention_kept[2 * pair : 2 * pair + 2].reshape(2 * length, length)
             attention = low.astype(f32)
             inner = jnp.sum(attention * g_attention, axis=-1, keepdims=True)
             g_scores = (attention * (g_attention - inner)).astype(bf16)
@@ -685,24 +687,24 @@
         d_out_ref[...] += dot(mixed[micro], middle[2 * micro + 1], 0, 0)
         d_qkv_ref[...] += dot(h_in[micro], packed[micro], 0, 0)
 
-    steps = max(2 * last + micro_count, last + 2 * micro_count)
+    warm = jnp.minimum(WARM * (last - stage), micro_count - 1)
+    steps = 2 * micro_count
 
     def step(index, carry):
-        f_micro = index - stage
-        b_micro = index - (2 * last - stage)
-        w_micro = index - jnp.maximum(stage + micro_count, 2 * last - stage)
-
-        @pl.when(jnp.logical_and(f_micro >= 0, f_micro < micro_count))
-        def _():
-            forward(f_micro)
+        b_micro = index - warm
+        w_micro = index - micro_count
+
+        @pl.when(index < micro_count)
+        def _():
+            forward(index)
+
+        @pl.when(w_micro >= 0)
+        def _():
+            weights(w_micro)
 
         @pl.when(jnp.logical_and(b_micro >= 0, b_micro < micro_count))
         def _():
             backward(b_micro)
-
-        @pl.when(jnp.logical_and(w_micro >= 0, w_micro < micro_count))
-        def _():
-            weights(w_micro)
 
         return carry
 
@@ -814,7 +816,7 @@
         block = jnp.concatenate(totals + [jnp.zeros((NORM_ROWS - 2, width), f32)], axis=0)
         for quarter in range(planes):
             start = (quarter * rows + kind) * NORM_ROWS
-            d_norm_ref[start : start + NORM_ROWS, :] = block
+            norm_full[start : start + NORM_ROWS, :] = block
 
     pl.semaphore_signal(
         core_free, inc=1, device_id={"section": partner[0], "dp": partner[1]}, device_id_type=MESH
@@ -826,6 +828,35 @@
             pl.semaphore_signal(
                 peer_free, inc=1, device_id={"section": far[0], "dp": far[1]}, device_id_type=MESH
             )
+
+    def direct_quarter(at_plane):
+        return jnp.where(at_plane < planes - 1, at_plane + 1, at_plane - 1)
+
+    def is_direct(pair):
+        return 2 * pair + core == direct_quarter(plane)
+
+    owns_direct = plane == direct_quarter(home_plane)
+
+    def direct_landing(matrix, from_row, at_row):
+        rows_of = pl.ds(at_row * heights[matrix], heights[matrix])
+        if from_row == 0:
+            return view(matrix, 3, rows_of)
+        return matrices[matrix][5].at[from_row - 1, rows_of, matrices[matrix][-1]]
+
+    def direct_args(matrix, pair, from_row, at_row):
+        return (
+            slot(matrix, 2 * rows * rows + pair * rows + at_row),
+            direct_landing(matrix, from_row, at_row),
+            peer_send.at[matrix, pair, at_row],
+            direct_recv.at[matrix, from_row, at_row],
+            (stage, 2 * pair + core),
+        )
+
+    def send_direct(matrix, pair, at_row):
+        for from_row in range(rows):
+            @pl.when(from_row == row)
+            def _():
+                remote_copy(*direct_args(matrix, pair, from_row, at_row)).start()
 
     def core_sum_args(matrix, pair, at_row):
         index = pair * rows + at_row
@@ -871,47 +902,85 @@
                 landed = slot(matrix, rows * rows + pair * rows + at_row)
                 part = view(matrix, 1, piece(matrix, 2 * pair + core, at_row))
                 total = part[...] + landed[...].astype(f32)
-
-                @pl.when(at_row != row)
+                direct = is_direct(pair)
+
+                @pl.when(direct)
+                def _():
+                    staged = slot(matrix, 2 * rows * rows + pair * rows + at_row)
+                    staged[...] = total.astype(staged.dtype)
+                    send_direct(matrix, pair, at_row)
+
+                @pl.when(jnp.logical_and(jnp.logical_not(direct), at_row != row))
                 def _():
                     args = peer_sum_args(matrix, pair, row, at_row)
                     args[0][...] = total.astype(args[0].dtype)
                     remote_copy(*args).start()
 
-                @pl.when(at_row == row)
+                @pl.when(jnp.logical_and(jnp.logical_not(direct), at_row == row))
                 def _():
                     part[...] = total
 
+    def give_total(matrix, pair):
+        part = view(matrix, 1, piece(matrix, 2 * pair + core, row))
+        for from_row in range(rows):
+            @pl.when(from_row != row)
+            def _():
+                remote_copy(*peer_sum_args(matrix, pair, from_row, from_row)).wait_recv()
+                landed = slot(matrix, 3 * rows * rows + pair * rows + from_row)
+                part[...] += landed[...].astype(f32)
+
+        args = total_args(matrix, pair)
+        args[0][...] = part[...].astype(args[0].dtype)
+        start_copy(*args, here)
+
     def give_totals(matrix):
         for pair in range(rows):
-            part = view(matrix, 1, piece(matrix, 2 * pair + core, row))
-            for from_row in range(rows):
-                @pl.when(from_row != row)
-                def _():
-                    remote_copy(*peer_sum_args(matrix, pair, from_row, from_row)).wait_recv()
-                    landed = slot(matrix, 3 * rows * rows + pair * rows + from_row)
-                    part[...] += landed[...].astype(f32)
-
-            args = total_args(matrix, pair)
-            args[0][...] = part[...].astype(args[0].dtype)
-            start_copy(*args, here)
+            @pl.when(jnp.logical_not(is_direct(pair)))
+            def _():
+                give_total(matrix, pair)
+
+    def sent(matrix, pair):
+        for at_row in range(rows):
+            @pl.when(at_row != row)
+            def _():
+                remote_copy(*peer_sum_args(matrix, pair, row, at_row)).wait_send()
+
+        wait_sent(*total_args(matrix, pair), here)
 
     def finish(matrix):
         height = heights[matrix]
-        for from_row in range(rows):
-            part = view(matrix, 3, pl.ds(from_row * height, height))
-            remote_copy(
-                part, part, total_send.at[matrix, 0], total_recv.at[matrix, from_row], partner
-            ).wait_recv()
+
+        @pl.when(owns_direct)
+        def _():
+            for at_row in range(rows):
+                for from_row in range(rows):
+                    remote_copy(*direct_args(matrix, 0, from_row, at_row)).wait_recv()
+                total = direct_landing(matrix, 0, at_row)
+                value = total[...].astype(f32)
+                for from_row in range(1, rows):
+                    value = value + direct_landing(matrix, from_row, at_row)[...].astype(f32)
+                total[...] = value.astype(total.dtype)
+
+        @pl.when(jnp.logical_not(owns_direct))
+        def _():
+            for from_row in range(rows):
+                part = view(matrix, 3, pl.ds(from_row * height, height))
+                remote_copy(
+                    part, part, total_send.at[matrix, 0], total_recv.at[matrix, from_row], partner
+                ).wait_recv()
+
         for pair in range(rows):
             for at_row in range(rows):
                 remote_copy(*core_sum_args(matrix, pair, at_row)).wait_send()
 
-                @pl.when(at_row != row)
-                def _():
-                    remote_copy(*peer_sum_args(matrix, pair, row, at_row)).wait_send()
-
-            wait_sent(*total_args(matrix, pair), here)
+            @pl.when(is_direct(pair))
+            def _():
+                for at_row in range(rows):
+                    remote_copy(*direct_args(matrix, pair, 0, at_row)).wait_send()
+
+            @pl.when(jnp.logical_not(is_direct(pair)))
+            def _():
+                sent(matrix, pair)
 
     order = tuple(reversed(range(count)))
     table_cores()
@@ -949,6 +1018,7 @@
     bf16, f32 = jnp.bfloat16, jnp.float32
     vmem = pl.BlockSpec(memory_space=pltpu.VMEM)
     anywhere = pl.BlockSpec(memory_space=pl.ANY)
+    scalars = pl.BlockSpec(memory_space=pltpu.SMEM)
     tokens = (micro_count, 3, length)
     norm_shard = (rows * NORM_ROWS, width)
     full = [(shard.shape[1] * planes, shard.shape[2]) for shard in shards]
@@ -965,7 +1035,7 @@
     return pl.pallas_call(
         functools.partial(pipeline_kernel, stages, planes),
         out_shape=outs,
-        in_specs=[vmem] * 6 + [anywhere] * 4,
+        in_specs=[vmem] * 2 + [scalars] + [vmem] * 3 + [anywhere] * 4,
         out_specs=[vmem] * 6 + [anywhere],
         scratch_shapes=[
             pltpu.VMEM(tokens, jnp.int32),
@@ -981,7 +1051,6 @@
             pltpu.VMEM((micro_count, length, hidden_units), bf16),
             pltpu.VMEM((micro_count, length, hidden_units), bf16),
             pltpu.VMEM((HEADS, length, length), bf16),
-            pltpu.VMEM((HEADS, length, length), bf16),
             pltpu.VMEM((length, width), f32),
             pltpu.VMEM((3, table_rows, width), bf16),
             pltpu.VMEM((4, 8, width), f32),
@@ -991,7 +1060,6 @@
             *(pltpu.VMEM(shape, bf16) for shape in full),
             pltpu.VMEM((NORM_ROWS, width), f32),
             pltpu.VMEM((NORM_ROWS, width), f32),
-            pltpu.VMEM(norm_full, f32),
             *(pltpu.VMEM(shape, f32) for shape in full),
             pltpu.SemaphoreType.DMA((2,)),
             pltpu.SemaphoreType.DMA((micro_count,)),
@@ -1016,9 +1084,12 @@
             pltpu.VMEM((2 + rows, table_rows, width), f32),
             pltpu.SemaphoreType.DMA((2 + rows + planes + stages // planes,)),
             pltpu.SemaphoreType.DMA((3 + rows,)),
+            pltpu.VMEM((rows - 1, *norm_shard), f32),
+            *(pltpu.VMEM((rows - 1, *shard.shape[1:]), bf16) for shard in shards),
+            pltpu.SemaphoreType.DMA(pieces),
         ],
         compiler_params=pltpu.CompilerParams(
-            vmem_limit_bytes=63 << 20, collective_id=0, has_side_effects=True
+            vmem_limit_bytes=(64 << 20) - (192 << 10), collective_id=0, has_side_effects=True
         ),
     )(token_ids, order, timesteps, table, gain, bias, w_qkv, w_out, w_in, w_down)
 

time: 350 us -> 337 us (0.963)
  Pallas kernels: 347 us -> 335 us
    pallas_call x1, Pallas kernels: 343 us -> 331 us  [run_pipeline(): pl.pallas_call(functools.partial(pipeline_kernel, stages, planes), out_sh...]
where the time goes in v5:
time: 337 us
  Pallas kernels  335 us (99%)
    pallas_call x1, Pallas kernels, run_pipeline(): pl.pallas_call(functools.partial(pipeline_kernel, stages, planes), out_sh...  331 us

profile of v5, /device:TPU:1, one launch (start us, length us, event | category | flops | bytes accessed | tf_op | source)
XLA Modules:
  0.0 337.2 jit_solution(8582333812432948817)
XLA Ops:
  0.6 1.3 copy.17.stamp_ref
  2.0 330.5 %shard_map.153 = (f32[32,512]{1,0:T(8,128)}, f32[16,512]{1,0:T(8,128)}, bf16[128,1536]{1,0:T(8,128)(2,1)}, bf16[128,512]{1,0:T(8,128)(2,1)}, bf16[128,2048]{1,0:...) custom-call(s32[8,1,256]{2,1,0:T(1,128)} %ids_ref.1, s32[8,1,256]{2,1,0:T(1,128)} %order_ref.1, ...), custom_call_target="tpu_custom_call" | custom-call | tf_op jit(solution)/shard_map/pallas_call | solution.py:1035
  332.5 4.6 %shard_map.154 = (f32[28,64]{1,0:T(8,128)}, f32[1,2,128]{2,1,0:T(2,128)}, f32[1,2,128]{2,1,0:T(2,128)}, f32[1,128,1536]{2,1,0:T(8,128)}, f32[1,128,512]{2,1,0:T(...) custom-call(f32[32,512]{1,0:T(8,128)} %get-tuple-element.13.refs_0_, f32[16,512]{1,0:T(8,128)} %get-tuple-element.14.refs_1_, ...), custom_call_target="tpu_custom_call" | custom-call | tf_op jit(solution)/shard_map/pallas_call | solution.py:1135

commit v6 on v5

--- a/solution.py
+++ b/solution.py
@@ -274,6 +274,9 @@
             inside = inside * height
         return buffer.at[block, pl.ds(inside, height), matrices[matrix][-1]]
 
+    def transit(matrix, index):
+        return slot(matrix, 2 * (matrices[matrix][4].shape[1] // heights[matrix]) + index)
+
     def piece(matrix, quarter, at_row):
         height = heights[matrix]
         return pl.ds(pl.multiple_of((quarter * rows + at_row) * height, height), height)
@@ -293,7 +296,7 @@
     for micro in range(micro_count):
         token_in_ref[micro, 0:1, :] = ids_ref[micro]
         token_in_ref[micro, 1:2, :] = order_ref[micro]
-        token_in_ref[micro, 2:3, :] = jnp.full((1, length), stamp_ref[micro, 0], jnp.int32)
+        token_in_ref[micro, 2:3, :] = jnp.full((1, length), stamp_ref[micro], jnp.int32)
     norm_shard[...] = jnp.zeros_like(norm_shard)
     share = gain_shard.shape[2]
     columns = lax.broadcasted_iota(jnp.int32, (2, width), 1)
@@ -316,7 +319,7 @@
         loads[matrix].wait()
         for at_row in range(rows):
             source = view(matrix, 1, pl.ds(at_row * heights[matrix], heights[matrix]))
-            slot(matrix, planes + at_row)[...] = source[...].astype(bf16)
+            transit(matrix, planes + at_row)[...] = source[...].astype(bf16)
     pl.semaphore_wait(barrier, sum(greetings))
 
     gives_tokens = jnp.logical_and(place == 0, lane_index == plane)
@@ -341,10 +344,10 @@
         if matrix == norms:
             source = norm_shard.at[pl.ds(at_row * NORM_ROWS, NORM_ROWS)]
         else:
-            source = slot(matrix, planes + at_row)
+            source = transit(matrix, planes + at_row)
         return (
             source,
-            slot(matrix, home_plane),
+            transit(matrix, home_plane),
             spread_send.at[matrix, at_row],
             spread_recv.at[matrix, home_plane],
             (target, plane),
@@ -352,7 +355,7 @@
 
     def plane_args(matrix, to_plane, from_plane):
         return (
-            slot(matrix, to_plane),
+            transit(matrix, to_plane),
             view(matrix, 0, piece(matrix, from_plane, row)),
             plane_send.at[matrix, to_plane],
             plane_recv.at[matrix, lax.div(from_plane, 2)],
@@ -387,9 +390,10 @@
         @pl.when(carries)
         def _():
             for to_plane in range(planes):
+                landed = transit(matrix, to_plane)
                 remote_copy(
-                    slot(matrix, to_plane),
-                    slot(matrix, to_plane),
+                    landed,
+                    landed,
                     spread_send.at[matrix, 0],
                     spread_recv.at[matrix, to_plane],
                     partner,
@@ -435,34 +439,6 @@
                     remote_copy(*peer_args(matrix, pair, row, at_row)).wait_send()
 
                 remote_copy(*core_args(matrix, pair, at_row, core)).wait_send()
-
-    steps_of_gather = (spread, along_planes, between_peers, between_cores, gathered)
-    order = (norms, *range(norms))
-    for turn_at in range(count + len(steps_of_gather) - 1):
-        for depth, action in enumerate(steps_of_gather):
-            if 0 <= turn_at - depth < count:
-                action(order[turn_at - depth])
-        if 1 <= turn_at <= 4:
-            sums = (d_qkv_ref, d_out_ref, d_in_ref, d_down_ref)[turn_at - 1]
-            sums[...] = jnp.zeros_like(sums)
-    for matrix in range(count):
-        gather_sent(matrix)
-
-    @pl.when(takes_tokens)
-    def _():
-        remote_copy(*token_copy(0, 0)).wait_recv()
-
-    @pl.when(gives_tokens)
-    def _():
-        for index, target in enumerate((0, planes - 1)):
-            wait_sent(*token_copy(index, target), here)
-
-    for kind, ref in enumerate((gain_ref, bias_ref)):
-        total = jnp.zeros((NORM_ROWS, width), f32)
-        for quarter in range(planes):
-            start = (quarter * rows + kind) * NORM_ROWS
-            total = total + norm_full[start : start + NORM_ROWS, :]
-        ref[...] = total.astype(bf16).astype(f32)
 
     letters = lax.broadcasted_iota(jnp.int32, (table_rows, length), 0)
     lane = lax.broadcasted_iota(jnp.int32, (length, pair_width), 1)
@@ -515,11 +491,7 @@
             device_id_type=MESH,
         )
 
-    def forward(micro):
-        if stages > 1:
-            @pl.when(stage > 0)
-            def _():
-                hidden_copy(micro, behind).wait_recv()
+    def forward_attention(micro):
         load_hidden(micro)
         hidden = work[...]
         unit, _ = unit_rows(hidden)
@@ -551,15 +523,16 @@
             mixed[micro, :, at : at + pair_width] = jnp.where(
                 lower, found[:length], found[length:]
             ).astype(bf16)
-        save = pltpu.make_async_copy(attention_kept, stash_ref.at[micro], stash_sem)
-        save.start()
+        pltpu.make_async_copy(attention_kept, stash_ref.at[micro], stash_sem).start()
         between = hidden + dot(mixed[micro], w_out_ref[...], 1, 0)
         high = between.astype(bf16)
         middle[2 * micro + 0] = high
         middle[2 * micro + 1] = (between - high.astype(f32)).astype(bf16)
         work[...] = between
         unit, _ = unit_rows(between)
-        normed_two = (unit * gain_ref[1:2, :] + bias_ref[1:2, :]).astype(bf16)
+        return (unit * gain_ref[1:2, :] + bias_ref[1:2, :]).astype(bf16)
+
+    def forward_lift(micro, normed_two):
         for at in range(0, hidden_units, FF_CHUNK):
             lifted = dot(normed_two, w_in_ref[:, at : at + FF_CHUNK], 1, 0)
             bent = (root * 0.044715) * (lifted * lifted)
@@ -569,6 +542,7 @@
             slope[micro, :, at : at + FF_CHUNK] = (
                 half + gelu * ((1.0 - half) * (6.0 * bent + 2.0 * root))
             ).astype(bf16)
+    def forward_end(micro):
         if stages > 1:
             @pl.when(jnp.logical_and(micro >= 2, stage < last))
             def _():
@@ -579,7 +553,64 @@
             @pl.when(stage < last)
             def _():
                 hidden_copy(micro, ahead).start()
-        save.wait()
+        pltpu.make_async_copy(attention_kept, stash_ref.at[micro], stash_sem).wait()
+
+    def forward(micro):
+        if stages > 1:
+            @pl.when(stage > 0)
+            def _():
+                hidden_copy(micro, behind).wait_recv()
+
+        forward_lift(micro, forward_attention(micro))
+        forward_end(micro)
+
+    def set_norms():
+        for kind, ref in enumerate((gain_ref, bias_ref)):
+            total = jnp.zeros((NORM_ROWS, width), f32)
+            for quarter in range(planes):
+                start = (quarter * rows + kind) * NORM_ROWS
+                total = total + norm_full[start : start + NORM_ROWS, :]
+            ref[...] = total.astype(bf16).astype(f32)
+
+    out_unit, in_unit = 2, 4
+    steps_of_gather = (spread, along_planes, between_peers, between_cores, gathered)
+    order = (norms, *range(norms))
+    for turn_at in range(count + len(steps_of_gather) - 1):
+        for depth, action in enumerate(steps_of_gather):
+            if 0 <= turn_at - depth < count:
+                action(order[turn_at - depth])
+        done = turn_at - len(steps_of_gather) + 1
+        if done == 0:
+            set_norms()
+        if done == order.index(out_unit):
+            @pl.when(takes_tokens)
+            def _():
+                remote_copy(*token_copy(0, 0)).wait_recv()
+
+            @pl.when(stage == 0)
+            def _():
+                g_send[0] = forward_attention(0)
+
+        if done == order.index(in_unit):
+            @pl.when(stage == 0)
+            def _():
+                forward_lift(0, g_send[0])
+
+        if 1 <= turn_at <= 4:
+            sums = (d_qkv_ref, d_out_ref, d_in_ref, d_down_ref)[turn_at - 1]
+            sums[...] = jnp.zeros_like(sums)
+    @pl.when(stage == 0)
+    def _():
+        forward_end(0)
+
+    for matrix in range(count):
+        gather_sent(matrix)
+
+    @pl.when(gives_tokens)
+    def _():
+        for index, target in enumerate((0, planes - 1)):
+            wait_sent(*token_copy(index, target), here)
+
 
     def head(micro):
         unit, scale = unit_rows(h_send[lax.rem(micro, 2)].astype(f32))
@@ -694,7 +725,7 @@
         b_micro = index - warm
         w_micro = index - micro_count
 
-        @pl.when(index < micro_count)
+        @pl.when(jnp.logical_and(index < micro_count, jnp.logical_or(stage > 0, index > 0)))
         def _():
             forward(index)
 
@@ -1121,7 +1152,7 @@
 
 def run_finish(stages, planes, vocab, share, sums):
     f32 = jnp.float32
-    steps = 4
+    steps = 2
     whole = [pl.BlockSpec(value.shape, lambda i: (0, 0)) for value in sums[:2]]
     blocks = [
         pl.BlockSpec((value.shape[0] // steps, value.shape[1]), lambda i: (i, 0))
@@ -1158,7 +1189,7 @@
         planes,
         token_ids,
         order,
-        timesteps,
+        timesteps[:, 0],
         table,
         norm_gain,
         norm_bias,

time: 337 us -> 333 us (0.988)
  no operation moved by 1% of the time
where the time goes in v6:
time: 333 us
  Pallas kernels  332 us (100%)
    pallas_call x1, Pallas kernels, run_pipeline(): pl.pallas_call(functools.partial(pipeline_kernel, stages, planes), out_sh...  328 us

profile of v6, /device:TPU:1, one launch (start us, length us, event | category | flops | bytes accessed | tf_op | source)
XLA Modules:
  0.0 332.6 jit_solution(10851494753578313490)
XLA Ops:
  0.6 328.3 %shard_map.153 = (f32[32,512]{1,0:T(8,128)}, f32[16,512]{1,0:T(8,128)}, bf16[128,1536]{1,0:T(8,128)(2,1)}, bf16[128,512]{1,0:T(8,128)(2,1)}, bf16[128,2048]{1,0:...) custom-call(s32[8,1,256]{2,1,0:T(1,128)} %ids_ref.1, s32[8,1,256]{2,1,0:T(1,128)} %order_ref.1, ...), custom_call_target="tpu_custom_call" | custom-call | tf_op jit(solution)/shard_map/pallas_call | solution.py:1066
  329.0 3.5 %shard_map.154 = (f32[28,64]{1,0:T(8,128)}, f32[1,2,128]{2,1,0:T(2,128)}, f32[1,2,128]{2,1,0:T(2,128)}, f32[1,128,1536]{2,1,0:T(8,128)}, f32[1,128,512]{2,1,0:T(...) custom-call(f32[32,512]{1,0:T(8,128)} %get-tuple-element.13.refs_0_, f32[16,512]{1,0:T(8,128)} %get-tuple-element.14.refs_1_, ...), custom_call_target="tpu_custom_call" | custom-call | tf_op jit(solution)/shard_map/pallas_call | solution.py:1166

commit v7 on v6

--- a/solution.py
+++ b/solution.py
@@ -315,11 +315,13 @@
         rest = rest - rounded.astype(f32)
     norm_sums[...] = jnp.zeros_like(norm_sums)
     table_sum[...] = jnp.zeros_like(table_sum)
-    for matrix in range(norms):
+    def rounded(matrix):
         loads[matrix].wait()
         for at_row in range(rows):
             source = view(matrix, 1, pl.ds(at_row * heights[matrix], heights[matrix]))
             transit(matrix, planes + at_row)[...] = source[...].astype(bf16)
+
+    rounded(0)
     pl.semaphore_wait(barrier, sum(greetings))
 
     gives_tokens = jnp.logical_and(place == 0, lane_index == plane)
@@ -383,6 +385,8 @@
         )
 
     def spread(matrix):
+        if matrix not in (0, norms):
+            rounded(matrix)
         for at_row in range(rows):
             start_copy(*spread_args(matrix, at_row), here)
 
@@ -596,8 +600,8 @@
             def _():
                 forward_lift(0, g_send[0])
 
-        if 1 <= turn_at <= 4:
-            sums = (d_qkv_ref, d_out_ref, d_in_ref, d_down_ref)[turn_at - 1]
+        if 7 <= turn_at <= 10:
+            sums = (d_qkv_ref, d_out_ref, d_in_ref, d_down_ref)[turn_at - 7]
             sums[...] = jnp.zeros_like(sums)
     @pl.when(stage == 0)
     def _():
@@ -1016,7 +1020,7 @@
     order = tuple(reversed(range(count)))
     table_cores()
     pl.semaphore_wait(core_free, 1)
-    for position in range(count + 3):
+    for position in range(count + 4):
         if position < count:
             give_core(order[position])
         if position == 1:
@@ -1024,8 +1028,8 @@
             pl.semaphore_wait(peer_free, rows - 1)
         if 0 <= position - 1 < count:
             give_peers(order[position - 1])
-        if 0 <= position - 3 < count:
-            give_totals(order[position - 3])
+        if 0 <= position - 4 < count:
+            give_totals(order[position - 4])
         if position == 4:
             table_down()
 

time: 333 us -> 330 us (level)
  no operation moved by 1% of the time
where the time goes in v7:
time: 330 us
  Pallas kernels  329 us (100%)
    pallas_call x1, Pallas kernels, run_pipeline(): pl.pallas_call(functools.partial(pipeline_kernel, stages, planes), out_sh...  326 us

profile of v7, /device:TPU:1, one launch (start us, length us, event | category | flops | bytes accessed | tf_op | source)
XLA Modules:
  0.0 330.2 jit_solution(9038950245564239850)
XLA Ops:
  0.6 325.9 %shard_map.153 = (f32[32,512]{1,0:T(8,128)}, f32[16,512]{1,0:T(8,128)}, bf16[128,1536]{1,0:T(8,128)(2,1)}, bf16[128,512]{1,0:T(8,128)(2,1)}, bf16[128,2048]{1,0:...) custom-call(s32[8,1,256]{2,1,0:T(1,128)} %ids_ref.1, s32[8,1,256]{2,1,0:T(1,128)} %order_ref.1, ...), custom_call_target="tpu_custom_call" | custom-call | tf_op jit(solution)/shard_map/pallas_call | solution.py:1070
  326.5 3.5 %shard_map.154 = (f32[28,64]{1,0:T(8,128)}, f32[1,2,128]{2,1,0:T(2,128)}, f32[1,2,128]{2,1,0:T(2,128)}, f32[1,128,1536]{2,1,0:T(8,128)}, f32[1,128,512]{2,1,0:T(...) custom-call(f32[32,512]{1,0:T(8,128)} %get-tuple-element.13.refs_0_, f32[16,512]{1,0:T(8,128)} %get-tuple-element.14.refs_1_, ...), custom_call_target="tpu_custom_call" | custom-call | tf_op jit(solution)/shard_map/pallas_call | solution.py:1170

commit v8 on v7

--- a/solution.py
+++ b/solution.py
@@ -579,11 +579,12 @@
     out_unit, in_unit = 2, 4
     steps_of_gather = (spread, along_planes, between_peers, between_cores, gathered)
     order = (norms, *range(norms))
-    for turn_at in range(count + len(steps_of_gather) - 1):
-        for depth, action in enumerate(steps_of_gather):
+    depths = (0, 1, 2, 4, 5)
+    for turn_at in range(count + depths[-1]):
+        for depth, action in zip(depths, steps_of_gather):
             if 0 <= turn_at - depth < count:
                 action(order[turn_at - depth])
-        done = turn_at - len(steps_of_gather) + 1
+        done = turn_at - depths[-1]
         if done == 0:
             set_norms()
         if done == order.index(out_unit):
@@ -695,8 +696,6 @@
         g_normed = dot(packed[micro], w_qkv_ref[...], 1, 1)
         unit, scale = unit_rows(work[...])
         h_in[micro] = (unit * gain_ref[0:1, :] + bias_ref[0:1, :]).astype(bf16)
-        norm_sums[0] += fold_rows(g_normed * unit)
-        norm_sums[2] += fold_rows(g_normed)
         g_hidden = g_middle + unit_back(g_normed * gain_ref[0:1, :], unit, scale)
 
         @pl.when(stage == 0)
@@ -715,6 +714,9 @@
 
                 g_send[lax.rem(micro, 2)] = g_hidden.astype(bf16)
                 gradient_copy(micro, behind).start()
+
+        norm_sums[0] += fold_rows(g_normed * unit)
+        norm_sums[2] += fold_rows(g_normed)
 
     def weights(micro):
         d_down_ref[...] += dot(active[micro], g_in[micro], 0, 0)
@@ -1156,7 +1158,7 @@
 
 def run_finish(stages, planes, vocab, share, sums):
     f32 = jnp.float32
-    steps = 2
+    steps = 1
     whole = [pl.BlockSpec(value.shape, lambda i: (0, 0)) for value in sums[:2]]
     blocks = [
         pl.BlockSpec((value.shape[0] // steps, value.shape[1]), lambda i: (i, 0))

time: 330 us -> 331 us (level)
  no operation moved by 1% of the time
where the time goes in v8:
time: 331 us; the launch traced here: 330 us
  Pallas kernels  330 us (100%)
    pallas_call x1, Pallas kernels, run_pipeline(): pl.pallas_call(functools.partial(pipeline_kernel, stages, planes), out_sh...  326 us

profile of v8, /device:TPU:1, one launch (start us, length us, event | category | flops | bytes accessed | tf_op | source)
XLA Modules:
  0.0 330.4 jit_solution(13196954478850950362)
XLA Ops:
  0.6 326.2 %shard_map.153 = (f32[32,512]{1,0:T(8,128)}, f32[16,512]{1,0:T(8,128)}, bf16[128,1536]{1,0:T(8,128)(2,1)}, bf16[128,512]{1,0:T(8,128)(2,1)}, bf16[128,2048]{1,0:...) custom-call(s32[8,1,256]{2,1,0:T(1,128)} %ids_ref.1, s32[8,1,256]{2,1,0:T(1,128)} %order_ref.1, ...), custom_call_target="tpu_custom_call" | custom-call | tf_op jit(solution)/shard_map/pallas_call | solution.py:1072
  326.8 3.6 %shard_map.154 = (f32[28,64]{1,0:T(8,128)}, f32[1,2,128]{2,1,0:T(2,128)}, f32[1,2,128]{2,1,0:T(2,128)}, f32[1,128,1536]{2,1,0:T(8,128)}, f32[1,128,512]{2,1,0:T(...) custom-call(f32[32,512]{1,0:T(8,128)} %get-tuple-element.13.refs_0_, f32[16,512]{1,0:T(8,128)} %get-tuple-element.14.refs_1_, ...), custom_call_target="tpu_custom_call" | custom-call | tf_op jit(solution)/shard_map/pallas_call | solution.py:1172
